TPU v7x, 256 devices: a whole 4x4x8 slice. The times are simulated.
256 devices in a mesh: gx: 64 (over z, x, y_hi), gy: 4 (over y_lo, core).
Axes of the slice: x: 4, y: 4 (y_hi: 2, y_lo: 2; y = y_hi * 2 + y_lo), z: 8, core: 2. Of those that a mesh axis runs over, the one named last changes fastest.
Arguments:
- features: bfloat16 [1024, 64, 256], P(('gx', 'gy')), may hold values from -12 to 12, as said below
- occupancy: int32 [1024, 64], P(('gx', 'gy')), may hold values from 0 to 1, as said below
- neighbours: int32 [1024, 27], P(('gx', 'gy')), may hold values from 0 to 12, as said below
- send_list: int32 [256, 8, 1], P(('gx', 'gy')), may hold values from 0 to 3, as said below
- weight: bfloat16 [27, 256, 256], replicated, may hold values from -0.078125 to 0.078125
- gamma: float32 [256], replicated, may hold values from 0.1 to 1.9
- beta: float32 [256], replicated, may hold values from -3 to 3
- out_grad: bfloat16 [1024, 64, 256], P(('gx', 'gy')), may hold values from -6 to 6
Outputs:
- block_out: bfloat16 [1024, 64, 256], P(('gx', 'gy'))
- feature_grad: bfloat16 [1024, 64, 256], P(('gx', 'gy'))
- weight_grad: bfloat16 [27, 256, 256], replicated
- gamma_grad: float32 [256], replicated
- beta_grad: float32 [256], replicated
Inputs may be any that keep to these rules, and one draw needn't show every extreme that they name: `occupancy`: each device has between 2 and 4 live bricks, its first ones, and some device has all 4; voxels of the other bricks are 0. `neighbours`: values below 4 name a live brick of the same device, 4 + 1 d + h names halo place (d, h), and 12 names the zero brick; entry 13 of a live brick is the brick itself, and all entries of a brick that is not live are 12. `send_list`: for each device and direction, one live brick of that device. `features`: zero at voxels that are not occupied is not promised.
All inputs are finite; a program needn't handle non-finite values.
Results may differ from a plain program's by a relative error of at most 0.005.
Values may be sent and summed in bfloat16 or wider, within the bound.
A program may use at most 128 MiB of HBM per device.

v0:
```python
import jax
import jax.numpy as jnp
import numpy as np
from jax import lax
from jax.sharding import PartitionSpec as P

DIRECTION_ROWS = (-1, -1, -1, 0, 0, 1, 1, 1)
DIRECTION_COLUMNS = (-1, 0, 1, -1, 1, -1, 0, 1)
BRICK_PICK = np.array([0, 1, 1, 1, 1, 2])
VOXEL_PICK = np.array([3, 0, 1, 2, 3, 0])
EPSILON = 1e-05


def shifted(value, axis, steps):
    count = lax.axis_size(axis)
    first, last = (max(0, -steps), min(count, count - steps))
    return lax.ppermute(value, axis, [(source, source + steps) for source in range(first, last)])


def assemble(extended, neighbour_table):
    brick_count = neighbour_table.shape[0]
    channels = extended.shape[-1]
    nearby = extended[neighbour_table].reshape(brick_count, 3, 3, 3, 4, 4, 4, channels)
    return nearby[
        :,
        BRICK_PICK[:, None, None],
        BRICK_PICK[None, :, None],
        BRICK_PICK[None, None, :],
        VOXEL_PICK[:, None, None],
        VOXEL_PICK[None, :, None],
        VOXEL_PICK[None, None, :],
        :,
    ]


def unfold(padded):
    brick_count = padded.shape[0]
    channels = padded.shape[-1]
    pieces = [
        padded[:, shift_x : shift_x + 4, shift_y : shift_y + 4, shift_z : shift_z + 4, :]
        for shift_x in range(3)
        for shift_y in range(3)
        for shift_z in range(3)
    ]
    return jnp.concatenate(pieces, axis=-1).reshape(brick_count * 64, 27 * channels)


def fold_back(column_grad, brick_count, channels):
    blocks = column_grad.reshape(brick_count, 4, 4, 4, 27, channels)
    padded = jnp.zeros((brick_count, 6, 6, 6, channels), jnp.float32)
    for shift_x in range(3):
        for shift_y in range(3):
            for shift_z in range(3):
                padded = padded.at[
                    :, shift_x : shift_x + 4, shift_y : shift_y + 4, shift_z : shift_z + 4, :
                ].add(blocks[:, :, :, :, 9 * shift_x + 3 * shift_y + shift_z, :])
    return padded


def spread_back(padded_grad, neighbour_table, slot_count):
    brick_count = neighbour_table.shape[0]
    channels = padded_grad.shape[-1]
    nearby = jnp.zeros((brick_count, 3, 3, 3, 4, 4, 4, channels), jnp.float32)
    nearby = nearby.at[
        :,
        BRICK_PICK[:, None, None],
        BRICK_PICK[None, :, None],
        BRICK_PICK[None, None, :],
        VOXEL_PICK[:, None, None],
        VOXEL_PICK[None, :, None],
        VOXEL_PICK[None, None, :],
        :,
    ].set(padded_grad)
    nearby = nearby.reshape(brick_count * 27, 64 * channels)
    selector = (
        neighbour_table.reshape(-1)[None, :] == jnp.arange(slot_count, dtype=jnp.int32)[:, None]
    ).astype(jnp.float32)
    summed = jnp.dot(selector, nearby, precision=lax.Precision.HIGHEST)
    return summed.reshape(slot_count, 64, channels)


def take_back(returned, chosen, brick_count):
    channels = returned.shape[-1]
    selector = (
        chosen.reshape(-1)[None, :] == jnp.arange(brick_count, dtype=jnp.int32)[:, None]
    ).astype(jnp.float32)
    flat = returned.reshape(-1, 64 * channels).astype(jnp.float32)
    return jnp.dot(selector, flat, precision=lax.Precision.HIGHEST).reshape(
        brick_count, 64, channels
    )


def on_device(features, occupancy, neighbours, send_list, weight, gamma, beta, out_grad):
    bricks = features.shape[0]
    channels = features.shape[-1]
    halo_slots = send_list.shape[2]
    slot_count = bricks + 8 * halo_slots + 1
    lookup = {}
    for direction in range(8):
        lookup[DIRECTION_ROWS[direction], DIRECTION_COLUMNS[direction]] = direction
    occupied = occupancy.astype(jnp.float32)[:, :, None]
    masked = features * occupancy.astype(jnp.bfloat16)[:, :, None]
    chosen = send_list[0]
    packets = masked[chosen]
    arrived = []
    for direction in range(8):
        parcel = packets[direction]
        if DIRECTION_ROWS[direction] != 0:
            parcel = shifted(parcel, "gx", DIRECTION_ROWS[direction])
        if DIRECTION_COLUMNS[direction] != 0:
            parcel = shifted(parcel, "gy", DIRECTION_COLUMNS[direction])
        arrived.append(parcel)
    halo_bricks = jnp.stack(arrived).reshape(8 * halo_slots, 64, channels)
    extended = jnp.concatenate(
        [masked, halo_bricks, jnp.zeros((1, 64, channels), jnp.bfloat16)], axis=0
    )
    columns = unfold(assemble(extended, neighbours))
    weight_rows = weight.reshape(27 * channels, channels)
    convolved = (
        jnp.dot(columns, weight_rows, preferred_element_type=jnp.float32).reshape(
            bricks, 64, channels
        )
        * occupied
    )
    local_count = jnp.sum(occupied)
    local_sum = jnp.sum(convolved, axis=(0, 1))
    voxel_count, channel_total = lax.psum((local_count, local_sum), ("gx", "gy"))
    average = channel_total / voxel_count
    centred = (convolved - average) * occupied
    spread = lax.psum(jnp.sum(centred * centred, axis=(0, 1)), ("gx", "gy"))
    variance = spread / voxel_count
    inverse_std = lax.rsqrt(variance + EPSILON)
    normalized = (convolved - average) * inverse_std
    normed = gamma * normalized + beta
    sigmoid_normed = jax.nn.sigmoid(normed)
    block_out = ((masked.astype(jnp.float32) + normed * sigmoid_normed) * occupied).astype(
        jnp.bfloat16
    )
    out_masked = out_grad.astype(jnp.float32) * occupied
    act_grad = out_masked * sigmoid_normed * (1.0 + normed * (1.0 - sigmoid_normed))
    grad_total, grad_cross = lax.psum(
        (jnp.sum(act_grad, axis=(0, 1)), jnp.sum(act_grad * normalized, axis=(0, 1))), ("gx", "gy")
    )
    conv_grad = (
        gamma
        * inverse_std
        * (act_grad - grad_total / voxel_count - normalized * grad_cross / voxel_count)
        * occupied
    ).astype(jnp.bfloat16)
    flat_up = conv_grad.reshape(bricks * 64, channels)
    local_weight = lax.dot_general(
        columns, flat_up, (((0,), (0,)), ((), ())), preferred_element_type=jnp.float32
    )
    inverse_root = lax.rsqrt(voxel_count)
    summed = lax.psum(local_weight, ("gx", "gy"))
    weight_grad = (summed * inverse_root).astype(jnp.bfloat16).reshape(27, channels, channels)
    column_grad = lax.dot_general(
        flat_up, weight_rows, (((1,), (1,)), ((), ())), preferred_element_type=jnp.float32
    )
    extended_grad = spread_back(fold_back(column_grad, bricks, channels), neighbours, slot_count)
    ghosts = (
        extended_grad[bricks : bricks + 8 * halo_slots]
        .astype(jnp.bfloat16)
        .reshape(8, halo_slots, 64, channels)
    )
    returned = []
    for direction in range(8):
        parcel = ghosts[direction]
        if DIRECTION_COLUMNS[direction] != 0:
            parcel = shifted(parcel, "gy", -DIRECTION_COLUMNS[direction])
        if DIRECTION_ROWS[direction] != 0:
            parcel = shifted(parcel, "gx", -DIRECTION_ROWS[direction])
        returned.append(parcel)
    extra = take_back(jnp.stack(returned), chosen, bricks)
    gradient_sum = out_masked + extended_grad[:bricks] + extra
    feature_grad = (gradient_sum * occupied).astype(jnp.bfloat16)
    return (
        block_out,
        feature_grad,
        weight_grad,
        grad_cross * inverse_root,
        grad_total * inverse_root,
    )


def solution(mesh):
    placed = (
        P(("gx", "gy"), None, None),
        P(("gx", "gy"), None),
        P(("gx", "gy"), None),
        P(("gx", "gy"), None, None),
        P(),
        P(),
        P(),
        P(("gx", "gy"), None, None),
    )
    return jax.shard_map(
        on_device,
        mesh=mesh,
        in_specs=placed,
        out_specs=(P(("gx", "gy"), None, None), P(("gx", "gy"), None, None), P(), P(), P()),
        check_vma=False,
    )
```

profile of v0, /device:TPU:1, one launch (start us, length us, event | category | flops | bytes accessed | tf_op | source)
XLA Modules:
  0.0 665.0 jit_solution(3921168128390595128)
XLA Ops:
  12.5 2.2 gather_fusion
  20.1 5.2 collective-permute-start.5
  25.3 1.9 collective-permute-start.6
  29.3 3.0 collective-permute-start.1
  35.8 7.0 %collective-permute-start.7 = (bf16[1,64,256]{2,1,0:T(8,128)(2,1)}, bf16[1,64,256]{2,1,0:T(8,128)(2,1)S(1)}, u32[]{:S(2)}, u32[]{:S(2)}) collective-permute-start(bf16[1,64,256]{2,1,0:T(8,128)(2,1)} %get-tuple-element.349), channel_id=1, source_target_pairs={{0,4},{4,8},{8,12},{12,16},{16,20},{20,24},{24,28},{28,32},{32,36}... | collective-permute-start | bytes 98312 | tf_op jit(solution)/shard_map/ppermute | solution.py:17
  43.6 6.0 collective-permute-start.10
  49.7 3.1 collective-permute-start.4
  53.6 5.2 collective-permute-start.9
  58.8 1.9 collective-permute-start.8
  60.7 3.6 collective-permute-start.11
  67.7 3.7 gather_fusion.1
  71.4 7.4 %reshape.1432 = bf16[4,3,3,3,4,4,4,256]{7,6,5,4,3,2,1,0:T(4,128)(2,1)} reshape(bf16[108,64,256]{2,1,0:T(8,128)(2,1)} %gather_fusion.1) | data formatting | bytes 7077888 | tf_op jit(solution)/shard_map/reshape | solution.py:23
  78.8 9.8 %copy.96 = bf16[4,3,3,3,4,4,4,256]{7,0,6,5,4,3,2,1:T(4,128)(2,1)} copy(bf16[4,3,3,3,4,4,4,256]{7,6,5,4,3,2,1,0:T(4,128)(2,1)} %reshape.1432) | data formatting | bytes 7077888 | tf_op jit(solution)/shard_map/reshape | solution.py:23
  88.6 7.0 %gather_fusion.2 = bf16[216,4,256]{2,1,0:T(4,128)(2,1)} fusion(bf16[4,3,3,3,4,4,4,256]{7,0,6,5,4,3,2,1:T(4,128)(2,1)} %copy.96, s32[216]{0:T(256)S(1)} %reshape.1483), kind=kCustom, calls=%fused_computation.2 | custom fusion | bytes 889920 | tf_op jit(solution)/shard_map/gather | solution.py:24
  110.2 12.0 %slice_dynamic-update-slice_fusion.2 = bf16[4,4,4,4,6912]{4,0,3,2,1:T(4,128)(2,1)S(1)} fusion(bf16[4,4,4,4,6912]{4,0,3,2,1:T(4,128)(2,1)S(1)} %slice_dynamic-update-slice_fusion.3, bf16[4,6,6,6,256]{4,0,3,2,1:T(4,128)(2,1)S(1)} %bitcast.283), kind=kLoop, calls=%fused_computation.88 | loop fusion | bytes 262144
  122.3 3.2 copy.127
  125.5 1.8 fusion.57
  127.3 79.6 %all-reduce.2 = (f32[256]{0:T(256)}, f32[]{:T(128)}) all-reduce(f32[256]{0:T(256)S(1)} %get-tuple-element.362, f32[]{:T(128)} %convert_reduce_fusion), channel_id=1, replica_groups=mesh['gx'=64,'gy'=4] {'gx','gy'}, use_global_device_ids=true, to_apply=%region_1.0 | all-reduce | flops 257 | bytes 2056 | tf_op jit(solution)/shard_map/psum | solution.py:127
  210.5 74.1 %psum.44 = f32[256]{0:T(256)} all-reduce(f32[256]{0:T(256)} %multiply_reduce_fusion.1), channel_id=1, replica_groups=mesh['gx'=64,'gy'=4] {'gx','gy'}, use_global_device_ids=true, to_apply=%region_5.0 | all-reduce | flops 256 | bytes 2048 | tf_op jit(solution)/shard_map/psum | solution.py:130
  284.6 6.6 reshape.1464
  291.2 1.9 fusion.53
  295.5 73.6 %all-reduce.1 = (f32[256]{0:T(256)}, f32[256]{0:T(256)}) all-reduce(f32[256]{0:T(256)} %get-tuple-element.338, f32[256]{0:T(256)} %get-tuple-element.337), channel_id=1, replica_groups=mesh['gx'=64,'gy'=4] {'gx','gy'}, use_global_device_ids=true, to_apply=%region_9.0 | all-reduce | flops 512 | bytes 4096 | tf_op jit(solution)/shard_map/psum | solution.py:141
  369.0 1.9 broadcast_multiply_fusion.1
  370.9 2.7 multiply_convert_fusion.1
  375.2 6.1 fusion.59
  381.3 2.1 fusion
  383.6 2.8 copy-done.3
  394.3 2.9 fusion.39
  397.2 3.4 scatter-add.99
  445.5 4.7 broadcast_in_dim.121
  450.2 26.1 %scatter_fusion = f32[4,3,3,3,4,4,4,256]{7,0,6,5,4,3,2,1:T(4,128)} fusion(f32[4,3,3,3,4,4,4,256]{7,0,6,5,4,3,2,1:T(4,128)} %broadcast_in_dim.121, s32[216]{0:T(256)S(1)} %reshape.1483, f32[216,4,256]{2,1,0:T(4,128)S(1)} %bitcast.286), kind=kCustom, calls=%fused_computation.3 | custom fusion | bytes 2659392 | tf_op jit(solution)/shard_map/scatter | solution.py:73
  476.4 8.0 %copy.125 = f32[4,3,3,3,4,4,4,256]{7,6,5,4,3,2,1,0:T(4,128)} copy(f32[4,3,3,3,4,4,4,256]{7,0,6,5,4,3,2,1:T(4,128)} %scatter_fusion) | data formatting | bytes 14155776 | tf_op jit(solution)/shard_map/scatter | solution.py:73
  484.3 9.8 %reshape.1463 = f32[108,16384]{1,0:T(8,128)} reshape(f32[4,3,3,3,4,4,4,256]{7,6,5,4,3,2,1,0:T(4,128)} %copy.125) | data formatting | bytes 14155776 | tf_op jit(solution)/shard_map/reshape | solution.py:74
  494.2 4.7 fusion.58
  500.3 3.2 collective-permute-start.12
  503.6 1.9 collective-permute-start.15
  505.5 3.6 collective-permute-start.19
  509.2 1.9 collective-permute-start.22
  511.2 4.4 collective-permute-start.14
  515.6 3.3 collective-permute-start.17
  518.9 1.9 collective-permute-start.18
  522.2 5.5 collective-permute-start.13
  527.7 3.7 collective-permute-start.16
  535.8 1.9 collective-permute-done.20
  537.7 1.9 collective-permute-done.23
  540.7 2.0 fusion.10
  542.7 109.8 %all-reduce.5.cloned.1.call-done = f32[6912,256]{1,0:T(8,128)} async-done(((f32[6912,256]{1,0:T(8,128)}), f32[6912,256]{1,0:T(8,128)}) %all-reduce.5.cloned.1.call-update) | async-done | bytes 7077904 | tf_op jit(solution)/shard_map/psum | solution.py:155
  652.5 5.4 multiply_convert_fusion
  (164 shorter events, 103.8 us)
Async XLA Ops:
  7.2 118.3 %copy-start = (bf16[27,256,256]{2,1,0:T(8,128)(2,1)S(1)}, bf16[27,256,256]{2,1,0:T(8,128)(2,1)}, u32[]{:S(2)}) copy-start(bf16[27,256,256]{2,1,0:T(8,128)(2,1)} %param.90) | copy-start | bytes 10616836
  7.2 645.3 %all-reduce.5.cloned.1.call-start = ((), (), s32[]{:S(2)}) async-start(), calls=%async_computation | async-start | bytes 14155776 | tf_op jit(solution)/shard_map/psum | solution.py:155
  16.2 13.0 %collective-permute-start = (bf16[1,64,256]{2,1,0:T(8,128)(2,1)S(1)}, bf16[1,64,256]{2,1,0:T(8,128)(2,1)}, u32[]{:S(2)}, u32[]{:S(2)}) collective-permute-start(bf16[1,64,256]{2,1,0:T(8,128)(2,1)S(1)} %get-tuple-element.354), channel_id=1, source_target_pairs={{4,0},{8,4},{12,8},{16,12},{20,16},{24,20},{28,24},{32,28},{36,32}... | collective-permute-start | bytes 98312 | tf_op jit(solution)/shard_map/ppermute | solution.py:17
  17.5 26.1 %collective-permute-start.2 = (bf16[1,64,256]{2,1,0:T(8,128)(2,1)}, bf16[1,64,256]{2,1,0:T(8,128)(2,1)}, u32[]{:S(2)}, u32[]{:S(2)}) collective-permute-start(bf16[1,64,256]{2,1,0:T(8,128)(2,1)} %get-tuple-element.353), channel_id=1, source_target_pairs={{4,0},{8,4},{12,8},{16,12},{20,16},{24,20},{28,24},{32,28},{36,32}... | collective-permute-start | bytes 98312 | tf_op jit(solution)/shard_map/ppermute | solution.py:17
  18.8 30.8 %collective-permute-start.3 = (bf16[1,64,256]{2,1,0:T(8,128)(2,1)}, bf16[1,64,256]{2,1,0:T(8,128)(2,1)}, u32[]{:S(2)}, u32[]{:S(2)}) collective-permute-start(bf16[1,64,256]{2,1,0:T(8,128)(2,1)} %get-tuple-element.352), channel_id=1, source_target_pairs={{4,0},{8,4},{12,8},{16,12},{20,16},{24,20},{28,24},{32,28},{36,32}... | collective-permute-start | bytes 98312 | tf_op jit(solution)/shard_map/ppermute | solution.py:17
  20.1 44.2 %collective-permute-start.5 = (bf16[1,64,256]{2,1,0:T(8,128)(2,1)}, bf16[1,64,256]{2,1,0:T(8,128)(2,1)}, u32[]{:S(2)}, u32[]{:S(2)}) collective-permute-start(bf16[1,64,256]{2,1,0:T(8,128)(2,1)} %get-tuple-element.351), channel_id=1, source_target_pairs={{1,0},{2,1},{3,2},{5,4},{6,5},{7,6},{9,8},{10,9},{11,10},{13,12},{... | collective-permute-start | bytes 98312 | tf_op jit(solution)/shard_map/ppermute | solution.py:17
  25.3 39.9 %collective-permute-start.6 = (bf16[1,64,256]{2,1,0:T(8,128)(2,1)}, bf16[1,64,256]{2,1,0:T(8,128)(2,1)}, u32[]{:S(2)}, u32[]{:S(2)}) collective-permute-start(bf16[1,64,256]{2,1,0:T(8,128)(2,1)} %get-tuple-element.350), channel_id=1, source_target_pairs={{0,1},{1,2},{2,3},{4,5},{5,6},{6,7},{8,9},{9,10},{10,11},{12,13},{... | collective-permute-start | bytes 98312 | tf_op jit(solution)/shard_map/ppermute | solution.py:17
  29.3 6.5 collective-permute-start.1
  35.8 17.8 %collective-permute-start.7 = (bf16[1,64,256]{2,1,0:T(8,128)(2,1)}, bf16[1,64,256]{2,1,0:T(8,128)(2,1)S(1)}, u32[]{:S(2)}, u32[]{:S(2)}) collective-permute-start(bf16[1,64,256]{2,1,0:T(8,128)(2,1)} %get-tuple-element.349), channel_id=1, source_target_pairs={{0,4},{4,8},{8,12},{12,16},{16,20},{20,24},{24,28},{28,32},{32,36}... | collective-permute-start | bytes 98312 | tf_op jit(solution)/shard_map/ppermute | solution.py:17
  43.6 15.2 %collective-permute-start.10 = (bf16[1,64,256]{2,1,0:T(8,128)(2,1)}, bf16[1,64,256]{2,1,0:T(8,128)(2,1)S(1)}, u32[]{:S(2)}, u32[]{:S(2)}) collective-permute-start(bf16[1,64,256]{2,1,0:T(8,128)(2,1)} %get-tuple-element.347), channel_id=1, source_target_pairs={{0,4},{4,8},{8,12},{12,16},{16,20},{20,24},{24,28},{28,32},{32,36}... | collective-permute-start | bytes 98312 | tf_op jit(solution)/shard_map/ppermute | solution.py:17
  49.7 11.0 %collective-permute-start.4 = (bf16[1,64,256]{2,1,0:T(8,128)(2,1)}, bf16[1,64,256]{2,1,0:T(8,128)(2,1)S(1)}, u32[]{:S(2)}, u32[]{:S(2)}) collective-permute-start(bf16[1,64,256]{2,1,0:T(8,128)(2,1)} %collective-permute-done.3), channel_id=1, source_target_pairs={{0,1},{1,2},{2,3},{4,5},{5,6},{6,7},{8,9},{9,10},{10,11},{12,13},{... | collective-permute-start | bytes 98312 | tf_op jit(solution)/shard_map/ppermute | solution.py:17
  53.6 12.4 %collective-permute-start.9 = (bf16[1,64,256]{2,1,0:T(8,128)(2,1)}, bf16[1,64,256]{2,1,0:T(8,128)(2,1)S(1)}, u32[]{:S(2)}, u32[]{:S(2)}) collective-permute-start(bf16[1,64,256]{2,1,0:T(8,128)(2,1)} %get-tuple-element.348), channel_id=1, source_target_pairs={{0,4},{4,8},{8,12},{12,16},{16,20},{20,24},{24,28},{28,32},{32,36}... | collective-permute-start | bytes 98312 | tf_op jit(solution)/shard_map/ppermute | solution.py:17
  58.8 7.1 %collective-permute-start.8 = (bf16[1,64,256]{2,1,0:T(8,128)(2,1)S(1)}, bf16[1,64,256]{2,1,0:T(8,128)(2,1)S(1)}, u32[]{:S(2)}, u32[]{:S(2)}) collective-permute-start(bf16[1,64,256]{2,1,0:T(8,128)(2,1)S(1)} %collective-permute-done.7), channel_id=1, source_target_pairs={{1,0},{2,1},{3,2},{5,4},{6,5},{7,6},{9,8},{10,9},{11,10},{13,12},{... | collective-permute-start | bytes 98312 | tf_op jit(solution)/shard_map/ppermute | solution.py:17
  60.7 5.2 collective-permute-start.11
  95.5 13.8 %copy-start.2 = (bf16[216,4,256]{2,1,0:T(4,128)(2,1)S(1)}, bf16[216,4,256]{2,1,0:T(4,128)(2,1)}, u32[]{:S(2)}) copy-start(bf16[216,4,256]{2,1,0:T(4,128)(2,1)} %gather_fusion.2) | copy-start | bytes 1327108
  293.1 0.6 copy-start.4
  383.4 2.9 copy-start.3
  484.3 9.8 %copy-start.6 = (s32[108]{0:T(128)S(1)}, s32[108]{0:T(128)}, u32[]{:S(2)}) copy-start(s32[108]{0:T(128)} %eq.30) | copy-start | bytes 1300
  494.2 39.9 %copy-start.5 = (f32[256]{0:T(256)S(1)}, f32[256]{0:T(256)}, u32[]{:S(2)}) copy-start(f32[256]{0:T(256)} %get-tuple-element.339) | copy-start | bytes 3076
  494.2 46.3 %copy-start.7 = (s32[1,8,1]{1,2,0:T(1,128)S(1)}, s32[1,8,1]{1,2,0:T(1,128)}, u32[]{:S(2)}) copy-start(s32[1,8,1]{1,2,0:T(1,128)} %param.89) | copy-start | bytes 100
  500.3 15.3 %collective-permute-start.12 = (bf16[1,64,256]{2,1,0:T(8,128)(2,1)S(1)}, bf16[1,64,256]{2,1,0:T(8,128)(2,1)S(1)}, u32[]{:S(2)}, u32[]{:S(2)}) collective-permute-start(bf16[1,64,256]{2,1,0:T(8,128)(2,1)S(1)} %slice.1574), channel_id=1, source_target_pairs={{0,1},{1,2},{2,3},{4,5},{5,6},{6,7},{8,9},{9,10},{10,11},{12,13},{... | collective-permute-start | bytes 98312 | tf_op jit(solution)/shard_map/ppermute | solution.py:17
  503.6 15.3 %collective-permute-start.15 = (bf16[1,64,256]{2,1,0:T(8,128)(2,1)S(1)}, bf16[1,64,256]{2,1,0:T(8,128)(2,1)S(1)}, u32[]{:S(2)}, u32[]{:S(2)}) collective-permute-start(bf16[1,64,256]{2,1,0:T(8,128)(2,1)S(1)} %slice.1578), channel_id=1, source_target_pairs={{1,0},{2,1},{3,2},{5,4},{6,5},{7,6},{9,8},{10,9},{11,10},{13,12},{... | collective-permute-start | bytes 98312 | tf_op jit(solution)/shard_map/ppermute | solution.py:17
  505.5 15.4 %collective-permute-start.19 = (bf16[1,64,256]{2,1,0:T(8,128)(2,1)S(1)}, bf16[1,64,256]{2,1,0:T(8,128)(2,1)S(1)}, u32[]{:S(2)}, u32[]{:S(2)}) collective-permute-start(bf16[1,64,256]{2,1,0:T(8,128)(2,1)S(1)} %slice.1584), channel_id=1, source_target_pairs={{0,1},{1,2},{2,3},{4,5},{5,6},{6,7},{8,9},{9,10},{10,11},{12,13},{... | collective-permute-start | bytes 98312 | tf_op jit(solution)/shard_map/ppermute | solution.py:17
  509.2 13.0 %collective-permute-start.22 = (bf16[1,64,256]{2,1,0:T(8,128)(2,1)S(1)}, bf16[1,64,256]{2,1,0:T(8,128)(2,1)S(1)}, u32[]{:S(2)}, u32[]{:S(2)}) collective-permute-start(bf16[1,64,256]{2,1,0:T(8,128)(2,1)S(1)} %slice.1588), channel_id=1, source_target_pairs={{1,0},{2,1},{3,2},{5,4},{6,5},{7,6},{9,8},{10,9},{11,10},{13,12},{... | collective-permute-start | bytes 98312 | tf_op jit(solution)/shard_map/ppermute | solution.py:17
  511.2 16.5 %collective-permute-start.14 = (bf16[1,64,256]{2,1,0:T(8,128)(2,1)S(1)}, bf16[1,64,256]{2,1,0:T(8,128)(2,1)S(1)}, u32[]{:S(2)}, u32[]{:S(2)}) collective-permute-start(bf16[1,64,256]{2,1,0:T(8,128)(2,1)S(1)} %slice.1576), channel_id=1, source_target_pairs={{0,4},{4,8},{8,12},{12,16},{16,20},{20,24},{24,28},{28,32},{32,36}... | collective-permute-start | bytes 98312 | tf_op jit(solution)/shard_map/ppermute | solution.py:17
  515.6 15.9 %collective-permute-start.17 = (bf16[1,64,256]{2,1,0:T(8,128)(2,1)S(1)}, bf16[1,64,256]{2,1,0:T(8,128)(2,1)S(1)}, u32[]{:S(2)}, u32[]{:S(2)}) collective-permute-start(bf16[1,64,256]{2,1,0:T(8,128)(2,1)S(1)} %slice.1580), channel_id=1, source_target_pairs={{0,1},{1,2},{2,3},{4,5},{5,6},{6,7},{8,9},{9,10},{10,11},{12,13},{... | collective-permute-start | bytes 98312 | tf_op jit(solution)/shard_map/ppermute | solution.py:17
  518.9 13.8 %collective-permute-start.18 = (bf16[1,64,256]{2,1,0:T(8,128)(2,1)S(1)}, bf16[1,64,256]{2,1,0:T(8,128)(2,1)S(1)}, u32[]{:S(2)}, u32[]{:S(2)}) collective-permute-start(bf16[1,64,256]{2,1,0:T(8,128)(2,1)S(1)} %slice.1582), channel_id=1, source_target_pairs={{1,0},{2,1},{3,2},{5,4},{6,5},{7,6},{9,8},{10,9},{11,10},{13,12},{... | collective-permute-start | bytes 98312 | tf_op jit(solution)/shard_map/ppermute | solution.py:17
  520.9 14.7 %collective-permute-start.21 = (bf16[1,64,256]{2,1,0:T(8,128)(2,1)S(1)}, bf16[1,64,256]{2,1,0:T(8,128)(2,1)S(1)}, u32[]{:S(2)}, u32[]{:S(2)}) collective-permute-start(bf16[1,64,256]{2,1,0:T(8,128)(2,1)S(1)} %slice.1586), channel_id=1, source_target_pairs={{4,0},{8,4},{12,8},{16,12},{20,16},{24,20},{28,24},{32,28},{36,32}... | collective-permute-start | bytes 98312 | tf_op jit(solution)/shard_map/ppermute | solution.py:17
  522.2 13.4 %collective-permute-start.13 = (bf16[1,64,256]{2,1,0:T(8,128)(2,1)S(1)}, bf16[1,64,256]{2,1,0:T(8,128)(2,1)S(1)}, u32[]{:S(2)}, u32[]{:S(2)}) collective-permute-start(bf16[1,64,256]{2,1,0:T(8,128)(2,1)S(1)} %collective-permute-done.12), channel_id=1, source_target_pairs={{0,4},{4,8},{8,12},{12,16},{16,20},{20,24},{24,28},{28,32},{32,36}... | collective-permute-start | bytes 98312 | tf_op jit(solution)/shard_map/ppermute | solution.py:17
  527.7 8.0 %collective-permute-start.16 = (bf16[1,64,256]{2,1,0:T(8,128)(2,1)S(1)}, bf16[1,64,256]{2,1,0:T(8,128)(2,1)S(1)}, u32[]{:S(2)}, u32[]{:S(2)}) collective-permute-start(bf16[1,64,256]{2,1,0:T(8,128)(2,1)S(1)} %collective-permute-done.15), channel_id=1, source_target_pairs={{0,4},{4,8},{8,12},{12,16},{16,20},{20,24},{24,28},{28,32},{32,36}... | collective-permute-start | bytes 98312 | tf_op jit(solution)/shard_map/ppermute | solution.py:17
  531.5 6.2 collective-permute-start.20
  532.8 6.8 %collective-permute-start.23 = (bf16[1,64,256]{2,1,0:T(8,128)(2,1)S(1)}, bf16[1,64,256]{2,1,0:T(8,128)(2,1)S(1)}, u32[]{:S(2)}, u32[]{:S(2)}) collective-permute-start(bf16[1,64,256]{2,1,0:T(8,128)(2,1)S(1)} %collective-permute-done.22), channel_id=1, source_target_pairs={{4,0},{8,4},{12,8},{16,12},{20,16},{24,20},{28,24},{32,28},{36,32}... | collective-permute-start | bytes 98312 | tf_op jit(solution)/shard_map/ppermute | solution.py:17
  540.7 117.2 %copy-start.1 = (bf16[27,256,256]{2,1,0:T(8,128)(2,1)S(1)}, bf16[27,256,256]{2,1,0:T(8,128)(2,1)}, u32[]{:S(2)}) copy-start(bf16[27,256,256]{2,1,0:T(8,128)(2,1)} %param.90) | copy-start | bytes 10616836
Sparse Core Ops, SparseCore 0:
  381.4 271.1 all-reduce.4
where the time goes:
time: 672 us; the launch traced here: 665 us
  blocking collectives  227 us (34%)
  local copies, waits for them, and re-layouts  162 us (24%)
  waiting for transfers between devices  114 us (17%)
  starting transfers between devices  74.3 us (11%)
  other arithmetic  56.7 us (8%)
  between operations  15.9 us (2%)
  matrix products  14.9 us (2%)
    psum x1, waiting for transfers between devices, on_device(): summed = lax.psum(local_weight, ('gx', 'gy'))  110 us
    psum x1, blocking collectives, on_device(): lax.psum((local_count, local_sum), ('gx', 'gy'))  79.6 us
    ppermute x24, starting transfers between devices, shifted(): lax.ppermute(value, axis, [(source, source + steps) for source in range(f...  74.3 us
    psum x1, blocking collectives, on_device(): spread = lax.psum(jnp.sum(centred * centred, axis=(0, 1)), ('gx', 'gy'))  74.1 us
    psum x1, blocking collectives, on_device(): lax.psum((jnp.sum(act_grad, axis=(0, 1)), jnp.sum(act_grad * normalized,...  73.6 us
    scatter x2, local copies, waits for them, and re-layouts, spread_back(): nearby = nearby.at[:, BRICK_PICK[:, None, None], BRICK_PICK[None, :, None...  34.1 us
    unnamed x57, local copies, waits for them, and re-layouts  33.4 us
    scatter-add x20, local copies, waits for them, and re-layouts, fold_back(): padded = padded.at[:, shift_x:shift_x + 4, shift_y:shift_y + 4, shift_z:s...  30.6 us
  transfers between devices with their start and end apart: 25, of which 3 were waited for; matrix products, arithmetic and copies ran while one was open for 19% of the time, Pallas kernels for 0%

commit v1 on v0

v1 whole, which is shorter than its diff:
```python
import functools

import jax
import jax.numpy as jnp
from jax import lax
from jax.experimental import pallas as pl
from jax.experimental.pallas import tpu as pltpu
from jax.sharding import PartitionSpec as P

Z, X, YH, YL = 8, 4, 2, 2
Y = YH * YL
PLANE = X * Y * 2

ROWS = (-1, -1, -1, 0, 0, 1, 1, 1)
COLUMNS = (-1, 0, 1, -1, 1, -1, 0, 1)
EPSILON = 1e-05
MESH = pl.DeviceIdType.MESH
F32, BF16, I32 = jnp.float32, jnp.bfloat16, jnp.int32

PARTS = ((0, 14, 0), (14, 13, 16))


def coordinates():
    gx, gy = lax.axis_index("gx"), lax.axis_index("gy")
    z = lax.div(gx, X * YH)
    x = lax.rem(lax.div(gx, YH), X)
    y = lax.rem(gx, YH) * YL + lax.div(gy, 2)
    return z, x, y, lax.rem(gy, 2)


def device(z, x, y, c):
    return (z * (X * YH) + x * YH + lax.div(y, YL), lax.rem(y, YL) * 2 + c)


def ahead(value, steps, count):
    return lax.rem(value + (steps + count) % count, count)


def dot(a, b):
    return jnp.dot(a, b, preferred_element_type=F32)


def place_row(p):
    return (p >= 1).astype(I32) + (p >= 5).astype(I32)


def kernel(
    occ_ref, nb_ref, send_ref, feat_ref, gamma_ref, beta_ref, og_ref, w_hbm,
    block_ref, fgrad_ref, wgrad_ref, ggrad_ref, bgrad_ref,
    tab, occn, masked, packets, ext, gath, slabs, weight, conv_s, norm_s, cols_t,
    pl1, zs1, pl2, zs2,
    cg_s, grad_s, ghosts, returned,
    own, osend, crecv, s1, r1, s2, r2, s3, r3, outb,
    w_sem, halo_s, halo_r, p1_s, p1_r, z1_s, z1_r, p2_s, p2_r, z2_s, z2_r,
    gh_s, gh_r, c_s, c_r, q1_s, q1_r, q2_s, q2_r, q3_s, q3_r, a3_s, a3_r, a2_s, a2_r, a1_s, a1_r, a0_s, a0_r, o_sem,
):
    z, x, y, c = coordinates()
    gx, gy = lax.axis_index("gx"), lax.axis_index("gy")
    ngx, ngy = Z * X * YH, YL * 2
    me = (x * Y + y) * 2 + c

    def neighbour(u, v):
        return (ahead(gx, u, ngx), ahead(gy, v, ngy))

    plane = [(dx, dy, dc) for dx in range(X) for dy in range(Y) for dc in range(2) if dx + dy + dc > 0]

    def plane_mate(step):
        dx, dy, dc = step
        return ahead(x, dx, X), ahead(y, dy, Y), ahead(c, dc, 2)

    barrier = pltpu.get_barrier_semaphore()
    greeted = 0
    for d in range(8):
        pl.semaphore_signal(barrier, inc=1, device_id=neighbour(ROWS[d], COLUMNS[d]), device_id_type=MESH)
        greeted += 1
    for step in plane:
        pl.semaphore_signal(barrier, inc=1, device_id=device(z, *plane_mate(step)), device_id_type=MESH)
        greeted += 1
    for dz in range(1, Z):
        pl.semaphore_signal(barrier, inc=1, device_id=device(ahead(z, dz, Z), x, y, c), device_id_type=MESH)
        greeted += 1

    weight_copy = pltpu.make_async_copy(w_hbm, weight, w_sem)
    weight_copy.start()

    tab[...] = jnp.zeros_like(tab)
    tab[0:4, 0:64] = occ_ref[...].astype(F32)
    tab[8:12, 0:27] = nb_ref[...].astype(F32)

    def pick(first, index):
        rows = [tab[first + n : first + n + 1, :] for n in range(4)]
        return jnp.where(index == 0, rows[0], jnp.where(index == 1, rows[1], jnp.where(index == 2, rows[2], rows[3])))

    def iotas(rows, lanes):
        shape = (rows, lanes)
        return lax.broadcasted_iota(I32, shape, 0), lax.broadcasted_iota(I32, shape, 1)

    ones = jnp.ones((128, 256), BF16)
    row, lane = iotas(256, 128)
    by_brick = jnp.where(lane == jnp.bitwise_and(row, 63), pick(0, jnp.right_shift(row, 6)), 0.0)
    occ_brick = dot(by_brick.astype(BF16), ones)
    feat = feat_ref[...].reshape(256, 256)
    masked_value = (feat.astype(F32) * occ_brick).astype(BF16)
    masked[...] = masked_value.reshape(4, 64, 256)
    ext[0:4] = masked_value.reshape(4, 64, 256)
    for d in range(8):
        packets[d] = masked[send_ref[0, d]]

    pl.semaphore_wait(barrier, greeted)
    halo = []
    for d in range(8):
        copy = pltpu.make_async_remote_copy(
            src_ref=packets.at[d], dst_ref=ext.at[4 + d], send_sem=halo_s.at[d], recv_sem=halo_r.at[d],
            device_id=neighbour(ROWS[d], COLUMNS[d]), device_id_type=MESH)
        copy.start()
        halo.append(copy)

    by_voxel = jnp.where(
        lane == jnp.right_shift(row, 4) * 4 + jnp.bitwise_and(row, 3),
        pick(0, jnp.bitwise_and(jnp.right_shift(row, 2), 3)), 0.0)
    occ = dot(by_voxel.astype(BF16), ones)
    occn[...] = occ
    row, lane = iotas(256, 256)
    order = jnp.bitwise_and(jnp.right_shift(row, 2), 3) * 64 + jnp.right_shift(row, 4) * 4 + jnp.bitwise_and(row, 3)
    to_rows = jnp.where(lane == order, occ, 0.0).astype(BF16)
    order = jnp.bitwise_and(jnp.right_shift(lane, 2), 3) * 64 + jnp.right_shift(lane, 4) * 4 + jnp.bitwise_and(lane, 3)
    to_bricks = jnp.where(row == order, 1.0, 0.0).astype(BF16)
    out_masked = dot(to_rows, og_ref[...].reshape(256, 256))

    table = tab[8:16, :]
    for d in range(8):
        u, v = ROWS[d], COLUMNS[d]
        missing = jnp.int32(0)
        if u != 0:
            missing = missing + (gx == (0 if u > 0 else ngx - 1)).astype(I32)
        if v != 0:
            missing = missing + (gy == (0 if v > 0 else ngy - 1)).astype(I32)
        table = jnp.where((table == 4.0 + d) & (missing > 0), 12.0, table)
    tab[8:16, :] = table
    row, lane = iotas(576, 128)
    pq = jnp.right_shift(row, 4)
    p = jnp.right_shift(pq * 43, 8)
    q = pq - 6 * p
    brick, w = jnp.bitwise_and(jnp.right_shift(row, 2), 3), jnp.bitwise_and(row, 3)
    places = 9 * place_row(p) + 3 * place_row(q)
    voxels = 16 * jnp.bitwise_and(p + 3, 3) + 4 * jnp.bitwise_and(q + 3, 3)
    near = pick(8, brick)
    lane_f = lane.astype(F32)
    for shift in range(3):
        cell = w + shift
        found = dot(jnp.where(lane == places + place_row(cell), near, 0.0).astype(BF16), jnp.ones((128, 128), BF16))
        source = found * 64.0 + (voxels + jnp.bitwise_and(cell + 3, 3)).astype(F32)
        for j in range(6):
            gath[shift, :, j * 128 : (j + 1) * 128] = jnp.where(source == lane_f + 128.0 * j, 1.0, 0.0).astype(BF16)

    for copy in halo:
        copy.wait()
    extended = ext[...].reshape(768, 256)
    for shift in range(3):
        slabs[shift] = dot(gath[shift], extended).astype(BF16)

    def columns(k):
        a, b, shift = k // 9, k // 3 % 3, k % 3
        return jnp.concatenate(
            [slabs[shift, (a + i) * 96 + b * 16 : (a + i) * 96 + b * 16 + 64, :] for i in range(4)], axis=0)

    weight_copy.wait()
    conv = dot(columns(0), weight[0])
    for k in range(1, 27):
        conv = conv + dot(columns(k), weight[k])
    conv = conv * occ

    def two(value):
        return jnp.concatenate([value[:, :128], value[:, 128:]], axis=0)

    def one(tile):
        return jnp.concatenate([tile[0:1, :], tile[1:2, :]], axis=1)

    def spread_plane(buffer, send, receive):
        copies = []
        for i, step in enumerate(plane):
            copy = pltpu.make_async_remote_copy(
                src_ref=buffer.at[me], dst_ref=buffer.at[me], send_sem=send.at[i], recv_sem=receive.at[i],
                device_id=device(z, *plane_mate(step)), device_id_type=MESH)
            copy.start()
            copies.append(copy)
        return copies

    def meet_plane(copies, buffer, send, receive):
        for i, step in enumerate(plane):
            dx, dy, dc = step
            place = (ahead(x, -dx, X) * Y + ahead(y, -dy, Y)) * 2 + ahead(c, -dc, 2)
            copies[i].wait_send()
            pltpu.make_async_remote_copy(
                src_ref=buffer.at[place], dst_ref=buffer.at[place], send_sem=send.at[i], recv_sem=receive.at[i],
                device_id=device(z, x, y, c), device_id_type=MESH).wait_recv()

    def spread_depth(buffer, send, receive):
        copies = []
        for dz in range(1, Z):
            copy = pltpu.make_async_remote_copy(
                src_ref=buffer.at[z], dst_ref=buffer.at[z], send_sem=send.at[dz - 1], recv_sem=receive.at[dz - 1],
                device_id=device(ahead(z, dz, Z), x, y, c), device_id_type=MESH)
            copy.start()
            copies.append(copy)
        return copies

    def meet_depth(copies, buffer, send, receive):
        for dz in range(1, Z):
            place = ahead(z, -dz, Z)
            copies[dz - 1].wait_send()
            pltpu.make_async_remote_copy(
                src_ref=buffer.at[place], dst_ref=buffer.at[place], send_sem=send.at[dz - 1],
                recv_sem=receive.at[dz - 1], device_id=device(z, x, y, c), device_id_type=MESH).wait_recv()

    def merge(buffer, count):
        tiles = [buffer[i] for i in range(count)]
        total = sum(tiles[1:], tiles[0])
        mean = total[0:2, :] / jnp.maximum(total[4:5, :], 1.0)
        square = total[2:4, :]
        for tile in tiles:
            gap = tile[0:2, :] / jnp.maximum(tile[4:5, :], 1.0) - mean
            square = square + tile[4:5, :] * gap * gap
        return total[0:2, :], square, total[4:5, :]

    def write(buffer, place, sums, squares, number):
        buffer[place] = jnp.concatenate([sums, squares, number, jnp.zeros((3, 128), F32)], axis=0)

    number = jnp.sum(occ, axis=0, keepdims=True)
    sums = jnp.sum(conv, axis=0, keepdims=True)
    centred = (conv - sums / jnp.maximum(number, 1.0)) * occ
    squares = jnp.sum(centred * centred, axis=0, keepdims=True)
    write(pl1, me, two(sums), two(squares), number[:, :128])
    copies = spread_plane(pl1, p1_s, p1_r)
    conv_s[...] = conv
    for k in range(14):
        cols_t[k] = columns(k).T
    meet_plane(copies, pl1, p1_s, p1_r)
    write(zs1, z, *merge(pl1, PLANE))
    copies = spread_depth(zs1, z1_s, z1_r)
    meet_depth(copies, zs1, z1_s, z1_r)
    sums, squares, number = merge(zs1, Z)
    voxel_count = jnp.concatenate([number, number], axis=1)
    average = one(sums) / voxel_count
    inverse_std = lax.rsqrt(one(squares) / voxel_count + EPSILON)
    gamma, beta = gamma_ref[...], beta_ref[...]
    occ = occn[...]
    normalized = (conv_s[...] - average) * inverse_std
    normed = gamma * normalized + beta
    sigmoid = 1.0 / (1.0 + jnp.exp(-normed))
    act_grad = out_masked * sigmoid * (1.0 + normed * (1.0 - sigmoid))
    total = jnp.sum(act_grad, axis=0, keepdims=True)
    cross = jnp.sum(act_grad * normalized, axis=0, keepdims=True)
    write(pl2, me, two(total), two(cross), jnp.zeros((1, 128), F32))
    copies = spread_plane(pl2, p2_s, p2_r)
    centre = columns(13).astype(F32)
    block = (occ * (centre + normed * sigmoid)).astype(BF16)
    block_ref[...] = dot(to_bricks, block).astype(BF16).reshape(4, 64, 256)
    norm_s[...] = normalized
    for k in range(14, 27):
        cols_t[k] = columns(k).T
    meet_plane(copies, pl2, p2_s, p2_r)
    tiles = pl2[0]
    for i in range(1, PLANE):
        tiles = tiles + pl2[i]
    zs2[z] = tiles
    copies = spread_depth(zs2, z2_s, z2_r)
    meet_depth(copies, zs2, z2_s, z2_r)
    tiles = zs2[0]
    for i in range(1, Z):
        tiles = tiles + zs2[i]
    total, cross = one(tiles[0:2]), one(tiles[2:4])
    inverse_root = lax.rsqrt(voxel_count)
    ggrad_ref[...] = cross * inverse_root
    bgrad_ref[...] = total * inverse_root
    conv_grad = (gamma * inverse_std * (act_grad - total / voxel_count - norm_s[...] * cross / voxel_count) * occ).astype(BF16)
    cg_s[...] = conv_grad

    mine = jnp.where(c == 0, conv_grad[:, :128].astype(F32), conv_grad[:, 128:].astype(F32)).astype(BF16)
    other = jnp.where(c == 0, conv_grad[:, 128:].astype(F32), conv_grad[:, :128].astype(F32)).astype(BF16)
    halves = jnp.concatenate([mine, other], axis=1)
    sister = device(z, x, y, 1 - c)
    core_copies = []
    for part, (first, count, _) in enumerate(PARTS):
        for k in range(first, first + count):
            product = dot(cols_t[k], halves)
            own[k] = product[:, :128]
            osend[k] = product[:, 128:].astype(BF16)
        copy = pltpu.make_async_remote_copy(
            src_ref=osend.at[pl.ds(first, count)], dst_ref=crecv.at[pl.ds(first, count)],
            send_sem=c_s.at[part], recv_sem=c_r.at[part], device_id=sister, device_id_type=MESH)
        copy.start()
        core_copies.append(copy)

    grad_s[...] = jnp.zeros_like(grad_s)

    def column_grad(k):
        a, b, shift = k // 9, k // 3 % 3, k % 3
        product = lax.dot_general(cg_s[...], weight[k], (((1,), (1,)), ((), ())), preferred_element_type=F32)
        for i in range(4):
            start = (a + i) * 96 + b * 16
            grad_s[shift, start : start + 64, :] += product[i * 64 : (i + 1) * 64, :]

    for k in range(27):
        column_grad(k)

    spans = ((x, X, y, Y), (y, Y, x, X))

    def mate(part, stage, step):
        along_x = (part == 0) == (stage == 1)
        if along_x:
            return device(z, ahead(x, step, X), y, c)
        return device(z, x, ahead(y, step, Y), c)

    stage1 = []
    for part, (first, count, _) in enumerate(PARTS):
        core_copies[part].wait()
        place, length, _, _ = spans[part]
        for k in range(first, first + count):
            value = own[k] + crecv[k].astype(F32)
            own[k] = value
            s1[k] = value.astype(BF16)
        for step in range(1, length):
            target = ahead(place, step, length)
            copy = pltpu.make_async_remote_copy(
                src_ref=s1.at[pl.ds(first, count), pl.ds(pl.multiple_of(target * (256 // length), 16), 256 // length)],
                dst_ref=r1.at[step - 1, pl.ds(first, count), pl.ds(0, 256 // length)],
                send_sem=q1_s.at[part, step - 1], recv_sem=q1_r.at[part, step - 1],
                device_id=mate(part, 1, step), device_id_type=MESH)
            copy.start()
            stage1.append(copy)

    def brick_grad(rows):
        result = None
        for shift in range(3):
            value = grad_s[shift]
            high = value.astype(BF16)
            low = (value - high.astype(F32)).astype(BF16)
            select = gath[shift, :, rows]
            for piece in (high, low):
                term = lax.dot_general(select, piece, (((0,), (0,)), ((), ())), preferred_element_type=F32)
                result = term if result is None else result + term
        return result

    ghosts[...] = brick_grad(slice(256, 768)).astype(BF16).reshape(8, 64, 256)
    back = []
    for d in range(8):
        copy = pltpu.make_async_remote_copy(
            src_ref=ghosts.at[d], dst_ref=returned.at[d], send_sem=gh_s.at[d], recv_sem=gh_r.at[d],
            device_id=neighbour(-ROWS[d], -COLUMNS[d]), device_id_type=MESH)
        copy.start()
        back.append(copy)
    out_bricks = dot(to_bricks, out_masked.astype(BF16))
    local = out_bricks + brick_grad(slice(0, 256))
    for copy in back:
        copy.wait()
    for b in range(4):
        extra = local[b * 64 : (b + 1) * 64, :]
        for d in range(8):
            extra = extra + jnp.where(send_ref[0, d] == b, returned[d].astype(F32), 0.0)
        fgrad_ref[b] = (extra * occ_brick[b * 64 : (b + 1) * 64, :]).astype(BF16)

    for copy in stage1:
        copy.wait()
    stage2 = []
    for part, (first, count, _) in enumerate(PARTS):
        place, length, place2, length2 = spans[part]
        rows, rows2 = 256 // length, 256 // length // length2
        for k in range(first, first + count):
            value = own[k, pl.ds(pl.multiple_of(place * rows, 16), rows), :]
            for step in range(1, length):
                value = value + r1[step - 1, k, 0:rows, :].astype(F32)
            own[k, 0:rows, :] = value
            s2[k, 0:rows, :] = value.astype(BF16)
        for step in range(1, length2):
            target = ahead(place2, step, length2)
            copy = pltpu.make_async_remote_copy(
                src_ref=s2.at[pl.ds(first, count), pl.ds(pl.multiple_of(target * rows2, 16), rows2)],
                dst_ref=r2.at[step - 1, pl.ds(first, count), pl.ds(0, rows2)],
                send_sem=q2_s.at[part, step - 1], recv_sem=q2_r.at[part, step - 1],
                device_id=mate(part, 2, step), device_id_type=MESH)
            copy.start()
            stage2.append(copy)
    for copy in stage2:
        copy.wait()
    depth = 16 // Z
    small = 256 // (X * Y)
    for part, (first, count, base) in enumerate(PARTS):
        _, _, place2, length2 = spans[part]
        for k in range(16):
            if k < count:
                value = own[first + k, pl.ds(pl.multiple_of(place2 * small, 16), small), :]
                for step in range(1, length2):
                    value = value + r2[step - 1, first + k].astype(F32)
            else:
                value = jnp.zeros((small, 128), F32)
            s3[k // depth, part * depth + k % depth] = value
    stage3 = []
    for dz in range(1, Z):
        copy = pltpu.make_async_remote_copy(
            src_ref=s3.at[ahead(z, dz, Z)], dst_ref=r3.at[dz - 1], send_sem=q3_s.at[dz - 1], recv_sem=q3_r.at[dz - 1],
            device_id=device(ahead(z, dz, Z), x, y, c), device_id_type=MESH)
        copy.start()
        stage3.append(copy)
    for copy in stage3:
        copy.wait()
    value = s3[z]
    for dz in range(1, Z):
        value = value + r3[dz - 1]
    value = (value * inverse_root[:, :128].reshape(1, 1, 128)).astype(BF16)

    half = pl.ds(pl.multiple_of(c * 128, 128), 128)
    row_a = pl.ds(pl.multiple_of(x * (256 // X) + y * small, 16), small)
    row_b = pl.ds(pl.multiple_of(y * (256 // Y) + x * small, 16), small)
    blocks = ((0, row_a), (16, row_b))
    for part, (base, rows) in enumerate(blocks):
        outb[pl.ds(base + z * depth, depth), rows, half] = value[part * depth : (part + 1) * depth]

    def push(where, send, receive, target):
        return pltpu.make_async_remote_copy(
            src_ref=outb.at[where], dst_ref=outb.at[where], send_sem=send, recv_sem=receive,
            device_id=target, device_id_type=MESH)

    here = device(z, x, y, c)
    sent = []
    for part, (base, rows) in enumerate(blocks):
        for dz in range(1, Z):
            copy = push((pl.ds(base + z * depth, depth), rows, half), a3_s.at[part, dz - 1], a3_r.at[part, dz - 1],
                        device(ahead(z, dz, Z), x, y, c))
            copy.start()
            sent.append(copy)
    for part, (base, rows) in enumerate(blocks):
        for dz in range(1, Z):
            push((pl.ds(base + ahead(z, -dz, Z) * depth, depth), rows, half), a3_s.at[part, dz - 1],
                 a3_r.at[part, dz - 1], here).wait_recv()
    for part, (first, count, base) in enumerate(PARTS):
        _, _, _, length2 = spans[part]
        for step in range(1, length2):
            copy = push((pl.ds(base, count), blocks[part][1], half), a2_s.at[part, step - 1], a2_r.at[part, step - 1],
                        mate(part, 2, step))
            copy.start()
            sent.append(copy)
    for part, (first, count, base) in enumerate(PARTS):
        place, length, place2, length2 = spans[part]
        for step in range(1, length2):
            start = place * (256 // length) + ahead(place2, -step, length2) * small
            push((pl.ds(base, count), pl.ds(pl.multiple_of(start, 16), small), half), a2_s.at[part, step - 1],
                 a2_r.at[part, step - 1], here).wait_recv()
    for part, (first, count, base) in enumerate(PARTS):
        place, length, place2, length2 = spans[part]
        span = pl.ds(pl.multiple_of(place * (256 // length), 16), 256 // length)
        for step in range(1, length):
            copy = push((pl.ds(base, count), span, half), a1_s.at[part, step - 1], a1_r.at[part, step - 1],
                        mate(part, 1, step))
            copy.start()
            sent.append(copy)
    for part, (first, count, base) in enumerate(PARTS):
        place, length, place2, length2 = spans[part]
        for step in range(1, length):
            start = ahead(place, -step, length) * (256 // length)
            push((pl.ds(base, count), pl.ds(pl.multiple_of(start, 16), 256 // length), half), a1_s.at[part, step - 1],
                 a1_r.at[part, step - 1], here).wait_recv()
    for part, (first, count, base) in enumerate(PARTS):
        copy = push((pl.ds(base, count), pl.ds(0, 256), half), a0_s.at[part], a0_r.at[part], sister)
        copy.start()
        sent.append(copy)
    other_half = pl.ds(pl.multiple_of((1 - c) * 128, 128), 128)
    last = []
    for part, (first, count, base) in enumerate(PARTS):
        push((pl.ds(base, count), pl.ds(0, 256), other_half), a0_s.at[part], a0_r.at[part], here).wait_recv()
        copy = pltpu.make_async_copy(outb.at[pl.ds(base, count)], wgrad_ref.at[pl.ds(first, count)], o_sem.at[part])
        copy.start()
        last.append(copy)
    for copy in sent:
        copy.wait_send()
    for copy in last:
        copy.wait()


def on_device(features, occupancy, neighbours, send_list, weight, gamma, beta, out_grad):
    vmem = pl.BlockSpec(memory_space=pltpu.VMEM)
    small = 256 // (X * Y)
    near, far = max(X, Y) - 1, Z - 1
    depth = 16 // Z
    dma = pltpu.SemaphoreType.DMA
    scratch = [
        pltpu.VMEM((16, 128), F32),
        pltpu.VMEM((256, 256), F32),
        pltpu.VMEM((4, 64, 256), BF16),
        pltpu.VMEM((8, 64, 256), BF16),
        pltpu.VMEM((12, 64, 256), BF16),
        pltpu.VMEM((3, 576, 768), BF16),
        pltpu.VMEM((3, 576, 256), BF16),
        pltpu.VMEM((27, 256, 256), BF16),
        pltpu.VMEM((256, 256), F32),
        pltpu.VMEM((256, 256), F32),
        pltpu.VMEM((27, 256, 256), BF16),
        pltpu.VMEM((PLANE, 8, 128), F32),
        pltpu.VMEM((Z, 8, 128), F32),
        pltpu.VMEM((PLANE, 8, 128), F32),
        pltpu.VMEM((Z, 8, 128), F32),
        pltpu.VMEM((256, 256), BF16),
        pltpu.VMEM((3, 576, 256), F32),
        pltpu.VMEM((8, 64, 256), BF16),
        pltpu.VMEM((8, 64, 256), BF16),
        pltpu.VMEM((27, 256, 128), F32),
        pltpu.VMEM((27, 256, 128), BF16),
        pltpu.VMEM((27, 256, 128), BF16),
        pltpu.VMEM((27, 256, 128), BF16),
        pltpu.VMEM((near, 27, 256 // min(X, Y), 128), BF16),
        pltpu.VMEM((27, 256 // min(X, Y), 128), BF16),
        pltpu.VMEM((near, 27, small, 128), BF16),
        pltpu.VMEM((Z, 2 * depth, small, 128), F32),
        pltpu.VMEM((far, 2 * depth, small, 128), F32),
        pltpu.VMEM((32, 256, 256), BF16),
        dma, dma((8,)), dma((8,)),
        dma((PLANE - 1,)), dma((PLANE - 1,)), dma((far,)), dma((far,)),
        dma((PLANE - 1,)), dma((PLANE - 1,)), dma((far,)), dma((far,)),
        dma((8,)), dma((8,)), dma((2,)), dma((2,)),
        dma((2, near)), dma((2, near)), dma((2, near)), dma((2, near)), dma((far,)), dma((far,)),
        dma((2, far)), dma((2, far)), dma((2, near)), dma((2, near)), dma((2, near)), dma((2, near)),
        dma((2,)), dma((2,)), dma((2,)),
    ]
    block, fgrad, wgrad, ggrad, bgrad = pl.pallas_call(
        kernel,
        name="brick_block",
        out_shape=(
            jax.ShapeDtypeStruct((4, 64, 256), BF16),
            jax.ShapeDtypeStruct((4, 64, 256), BF16),
            jax.ShapeDtypeStruct((27, 256, 256), BF16),
            jax.ShapeDtypeStruct((1, 256), F32),
            jax.ShapeDtypeStruct((1, 256), F32),
        ),
        in_specs=[vmem, vmem, pl.BlockSpec(memory_space=pltpu.SMEM), vmem, vmem, vmem, vmem,
                  pl.BlockSpec(memory_space=pl.ANY)],
        out_specs=(vmem, vmem, pl.BlockSpec(memory_space=pl.ANY), vmem, vmem),
        scratch_shapes=scratch,
        compiler_params=pltpu.CompilerParams(
            collective_id=0, has_side_effects=True, vmem_limit_bytes=56 * 2**20),
    )(occupancy, neighbours, send_list.reshape(1, 8), features, gamma.reshape(1, 256), beta.reshape(1, 256), out_grad, weight)
    return block, fgrad, wgrad, ggrad.reshape(256), bgrad.reshape(256)


def solution(mesh):
    placed = (
        P(("gx", "gy"), None, None),
        P(("gx", "gy"), None),
        P(("gx", "gy"), None),
        P(("gx", "gy"), None, None),
        P(),
        P(),
        P(),
        P(("gx", "gy"), None, None),
    )
    return jax.shard_map(
        on_device,
        mesh=mesh,
        in_specs=placed,
        out_specs=(P(("gx", "gy"), None, None), P(("gx", "gy"), None, None), P(), P(), P()),
        check_vma=False,
    )
```

time: 672 us -> 114 us (0.17); the launches traced: 665 us -> 114 us
  blocking collectives: 227 us -> 0 us
  local copies, waits for them, and re-layouts: 162 us -> 8.44 us
  waiting for transfers between devices: 114 us -> 0 us
  Pallas kernels: 0 us -> 105 us
  starting transfers between devices: 74.3 us -> 0 us
  other arithmetic: 56.7 us -> 0 us
  between operations: 15.9 us -> 0.65 us
  matrix products: 14.9 us -> 0 us
    psum x3 -> x0, blocking collectives: 227 us -> none  [the longest x1 79.6 us: on_device(): lax.psum((local_count, local_sum), ('gx', 'gy'))]
    psum x1 -> x0, waiting for transfers between devices: 110 us -> none  [on_device(): summed = lax.psum(local_weight, ('gx', 'gy'))]
    pallas_call x0 -> x1, Pallas kernels: none -> 105 us  [on_device(): pl.pallas_call(kernel, name='brick_block', out_shape=(jax.ShapeDtypeStruc...]
    ppermute x24 -> x0, starting transfers between devices: 74.3 us -> none  [shifted(): lax.ppermute(value, axis, [(source, source + steps) for source in range(f...]
    scatter x2 -> x0, local copies, waits for them, and re-layouts: 34.1 us -> none  [spread_back(): nearby = nearby.at[:, BRICK_PICK[:, None, None], BRICK_PICK[None, :, None...]
    reshape x4 -> x0, local copies, waits for them, and re-layouts: 33.6 us -> none  [the longest x2 17.1 us: assemble(): extended[neighbour_table].reshape(brick_count, 3, 3, 3, 4, 4, 4, channels)]
    scatter-add x20 -> x0, local copies, waits for them, and re-layouts: 30.6 us -> none  [fold_back(): padded = padded.at[:, shift_x:shift_x + 4, shift_y:shift_y + 4, shift_z:s...]
    unnamed x57 -> x9, local copies, waits for them, and re-layouts: 33.4 us -> 8.44 us
  transfers between devices with their start and end apart: 25 -> 0, of which waited for: 3 -> 0; matrix products, arithmetic and copies ran while one was open for 19% -> 0% of each run, Pallas kernels for 0% -> 0%
where the time goes in v1:
time: 114 us
  Pallas kernels  105 us (92%)
  local copies, waits for them, and re-layouts  8.44 us (7%)
    pallas_call x1, Pallas kernels, on_device(): pl.pallas_call(kernel, name='brick_block', out_shape=(jax.ShapeDtypeStruc...  105 us
    unnamed x9, local copies, waits for them, and re-layouts  8.44 us

profile of v1, /device:TPU:1, one launch (start us, length us, event | category | flops | bytes accessed | tf_op | source)
XLA Modules:
  0.0 114.2 jit_solution(17635979925324608896)
XLA Ops:
  0.6 105.1 %brick_block.1 = (bf16[4,64,256]{2,1,0:T(8,128)(2,1)}, bf16[4,64,256]{2,1,0:T(8,128)(2,1)}, bf16[27,256,256]{2,1,0:T(8,128)(2,1)}, f32[1,256]{1,0:T(1,128)}, f32[1,256]{1,0:T(1,128)}) custom-call(s32[4,64]{1,0:T(4,128)} %occ_ref.1, s32[4,27]{1,0:T(4,128)} %nb_ref.1, s32[1,8]{1,0:T(1,128)} %bitcast.9, bf16[4,64,256]{2,1,0:T(8,128)(2,1)} %feat_ref.1, ...), custom_call_target="tpu_custom_call" | custom-call | tf_op jit(solution)/shard_map/brick_block/pallas_call | solution.py:524
  105.7 1.6 %copy.18 = bf16[4,64,256]{2,1,0:T(8,128)(2,1)} copy(bf16[4,64,256]{2,1,0:T(8,128)(2,1)} %get-tuple-element.20) | data formatting | bytes 262144
  107.3 1.6 %copy.19 = bf16[4,64,256]{2,1,0:T(8,128)(2,1)} copy(bf16[4,64,256]{2,1,0:T(8,128)(2,1)} %get-tuple-element.21) | data formatting | bytes 262144
  108.9 0.0 copy-start.1
  108.9 0.0 copy-start
  108.9 4.2 %copy.20 = bf16[27,256,256]{2,1,0:T(8,128)(2,1)} copy(bf16[27,256,256]{2,1,0:T(8,128)(2,1)} %get-tuple-element.22) | data formatting | bytes 7077888
  113.1 0.0 copy-done.1
  113.1 0.6 copy.21
  113.6 0.0 copy-done
  113.6 0.6 copy.22
Async XLA Ops:
  108.9 4.2 %copy-start.1 = (f32[1,256]{1,0:T(1,128)S(1)}, f32[1,256]{1,0:T(1,128)}, u32[]{:S(2)}) copy-start(f32[1,256]{1,0:T(1,128)} %get-tuple-element.13) | copy-start | bytes 3076
  108.9 4.7 %copy-start = (f32[1,256]{1,0:T(1,128)S(1)}, f32[1,256]{1,0:T(1,128)}, u32[]{:S(2)}) copy-start(f32[1,256]{1,0:T(1,128)} %get-tuple-element.14) | copy-start | bytes 3076

commit v2 on v1

v2 whole, which is shorter than its diff:
```python
import functools

import jax
import jax.numpy as jnp
from jax import lax
from jax.experimental import pallas as pl
from jax.experimental.pallas import tpu as pltpu
from jax.sharding import PartitionSpec as P

Z, X, YH, YL = 8, 4, 2, 2
Y = YH * YL

ROWS = (-1, -1, -1, 0, 0, 1, 1, 1)
COLUMNS = (-1, 0, 1, -1, 1, -1, 0, 1)
EPSILON = 1e-05
MESH = pl.DeviceIdType.MESH
F32, BF16, I32 = jnp.float32, jnp.bfloat16, jnp.int32

PIECES = ((0, 8, True), (8, 8, False), (16, 6, True), (22, 5, False))


def coordinates():
    gx, gy = lax.axis_index("gx"), lax.axis_index("gy")
    z = lax.div(gx, X * YH)
    x = lax.rem(lax.div(gx, YH), X)
    y = lax.rem(gx, YH) * YL + lax.div(gy, 2)
    return z, x, y, lax.rem(gy, 2)


def device(z, x, y, c):
    return (z * (X * YH) + x * YH + lax.div(y, YL), lax.rem(y, YL) * 2 + c)


def ahead(value, steps, count):
    return lax.rem(value + (steps + count) % count, count)


def dot(a, b):
    return jnp.dot(a, b, preferred_element_type=F32)


def place_row(p):
    return (p >= 1).astype(I32) + (p >= 5).astype(I32)


def kernel(
    occ_hbm, nb_hbm, send_ref, feat_hbm, gamma_hbm, beta_hbm, og_hbm, w_hbm,
    block_ref, fgrad_ref, outb, ggrad_ref, bgrad_ref,
    occ_ref, nb_ref, feat_ref, gamma_ref, beta_ref, og_ref, tab, occn, masked, packets, ext, gath, gath_t, slabs, weight, conv_s, norm_s, cols_t,
    deep1, wide1, deep2, wide2,
    cg_s, grad_s, local_s, ghosts, returned,
    own, osend, crecv, s1, r1, s2, r2, s3, r3,
    in_sem, halo_s, halo_r, d1_s, d1_r, w1_s, w1_r, d2_s, d2_r, w2_s, w2_r,
    gh_s, gh_r, c_s, c_r, q1_s, q1_r, q2_s, q2_r, q3_s, q3_r, a3_s, a3_r, a2_s, a2_r, a1_s, a1_r, a0_s, a0_r,
):
    z, x, y, c = coordinates()
    gx, gy = lax.axis_index("gx"), lax.axis_index("gy")
    ngx, ngy = Z * X * YH, YL * 2

    def neighbour(u, v):
        return (ahead(gx, u, ngx), ahead(gy, v, ngy))

    deep_group = [
        (device(ahead(z, dz, Z), x, y, ahead(c, dc, 2)), ahead(z, -dz, Z) * 2 + ahead(c, dc, 2))
        for dz in range(Z) for dc in range(2) if dz + dc > 0]
    wide_group = [
        (device(z, ahead(x, dx, X), ahead(y, dy, Y), c), ahead(x, -dx, X) * Y + ahead(y, -dy, Y))
        for dx in range(X) for dy in range(Y) if dx + dy > 0]

    barrier = pltpu.get_barrier_semaphore()
    friends = [neighbour(ROWS[d], COLUMNS[d]) for d in range(8)]
    friends += [friend for friend, _ in deep_group + wide_group]
    for friend in friends:
        pl.semaphore_signal(barrier, inc=1, device_id=friend, device_id_type=MESH)

    inputs = [
        pltpu.make_async_copy(source, target, in_sem.at[i])
        for i, (source, target) in enumerate((
            (occ_hbm, occ_ref), (feat_hbm, feat_ref), (nb_hbm, nb_ref), (og_hbm, og_ref),
            (gamma_hbm, gamma_ref), (beta_hbm, beta_ref), (w_hbm, weight)))]
    for copy in inputs:
        copy.start()

    tab[...] = jnp.zeros_like(tab)
    inputs[0].wait()
    inputs[1].wait()
    tab[0:4, 0:64] = occ_ref[...].astype(F32)

    def pick(first, index):
        rows = [tab[first + n : first + n + 1, :] for n in range(4)]
        return jnp.where(index == 0, rows[0], jnp.where(index == 1, rows[1], jnp.where(index == 2, rows[2], rows[3])))

    def iotas(rows, lanes):
        shape = (rows, lanes)
        return lax.broadcasted_iota(I32, shape, 0), lax.broadcasted_iota(I32, shape, 1)

    ones = jnp.ones((128, 256), BF16)
    row, lane = iotas(256, 128)
    by_brick = jnp.where(lane == jnp.bitwise_and(row, 63), pick(0, jnp.right_shift(row, 6)), 0.0)
    occ_brick = dot(by_brick.astype(BF16), ones)
    feat = feat_ref[...].reshape(256, 256)
    masked_value = (feat.astype(F32) * occ_brick).astype(BF16)
    masked[...] = masked_value.reshape(4, 64, 256)
    ext[0:4] = masked_value.reshape(4, 64, 256)
    for d in range(8):
        packets[d] = masked[send_ref[0, d]]

    pl.semaphore_wait(barrier, len(friends))
    halo = []
    for d in range(8):
        copy = pltpu.make_async_remote_copy(
            src_ref=packets.at[d], dst_ref=ext.at[4 + d], send_sem=halo_s.at[d], recv_sem=halo_r.at[d],
            device_id=neighbour(ROWS[d], COLUMNS[d]), device_id_type=MESH)
        copy.start()
        halo.append(copy)

    for copy in inputs[2:6]:
        copy.wait()
    by_voxel = jnp.where(
        lane == jnp.right_shift(row, 4) * 4 + jnp.bitwise_and(row, 3),
        pick(0, jnp.bitwise_and(jnp.right_shift(row, 2), 3)), 0.0)
    occ = dot(by_voxel.astype(BF16), ones)
    occn[...] = occ
    row, lane = iotas(256, 256)
    order = jnp.bitwise_and(jnp.right_shift(row, 2), 3) * 64 + jnp.right_shift(row, 4) * 4 + jnp.bitwise_and(row, 3)
    to_rows = jnp.where(lane == order, occ, 0.0).astype(BF16)
    order = jnp.bitwise_and(jnp.right_shift(lane, 2), 3) * 64 + jnp.right_shift(lane, 4) * 4 + jnp.bitwise_and(lane, 3)
    to_bricks = jnp.where(row == order, 1.0, 0.0).astype(BF16)
    out_masked = dot(to_rows, og_ref[...].reshape(256, 256))

    tab[8:12, 0:27] = nb_ref[...].astype(F32)
    table = tab[8:16, :]
    for d in range(8):
        u, v = ROWS[d], COLUMNS[d]
        missing = jnp.int32(0)
        if u != 0:
            missing = missing + (gx == (0 if u > 0 else ngx - 1)).astype(I32)
        if v != 0:
            missing = missing + (gy == (0 if v > 0 else ngy - 1)).astype(I32)
        table = jnp.where((table == 4.0 + d) & (missing > 0), 12.0, table)
    tab[8:16, :] = table
    row, lane = iotas(576, 128)
    pq = jnp.right_shift(row, 4)
    p = jnp.right_shift(pq * 43, 8)
    q = pq - 6 * p
    brick, w = jnp.bitwise_and(jnp.right_shift(row, 2), 3), jnp.bitwise_and(row, 3)
    places = 9 * place_row(p) + 3 * place_row(q)
    voxels = 16 * jnp.bitwise_and(p + 3, 3) + 4 * jnp.bitwise_and(q + 3, 3)
    near = pick(8, brick)
    lane_f = lane.astype(F32)
    for shift in range(3):
        cell = w + shift
        found = dot(jnp.where(lane == places + place_row(cell), near, 0.0).astype(BF16), jnp.ones((128, 128), BF16))
        source = found * 64.0 + (voxels + jnp.bitwise_and(cell + 3, 3)).astype(F32)
        for j in range(6):
            gath[shift, :, j * 128 : (j + 1) * 128] = jnp.where(source == lane_f + 128.0 * j, 1.0, 0.0).astype(BF16)

    for copy in halo:
        copy.wait()
    extended = ext[...].reshape(768, 256)
    for shift in range(3):
        slabs[shift] = dot(gath[shift], extended).astype(BF16)

    def columns(k):
        a, b, shift = k // 9, k // 3 % 3, k % 3
        return jnp.concatenate(
            [slabs[shift, (a + i) * 96 + b * 16 : (a + i) * 96 + b * 16 + 64, :] for i in range(4)], axis=0)

    inputs[6].wait()
    conv = dot(columns(0), weight[0])
    for k in range(1, 27):
        conv = conv + dot(columns(k), weight[k])
    conv = conv * occ

    def two(value):
        return jnp.concatenate([value[:, :128], value[:, 128:]], axis=0)

    def one(tile):
        return jnp.concatenate([tile[0:1, :], tile[1:2, :]], axis=1)

    def spread(buffer, place, group, send, receive):
        copies = []
        for i, (friend, _) in enumerate(group):
            copy = pltpu.make_async_remote_copy(
                src_ref=buffer.at[place], dst_ref=buffer.at[place], send_sem=send.at[i], recv_sem=receive.at[i],
                device_id=friend, device_id_type=MESH)
            copy.start()
            copies.append(copy)
        return copies

    def meet(copies, buffer, group, send, receive):
        for i, (friend, behind) in enumerate(group):
            pltpu.make_async_remote_copy(
                src_ref=buffer.at[behind], dst_ref=buffer.at[behind], send_sem=send.at[i], recv_sem=receive.at[i],
                device_id=friend, device_id_type=MESH).wait_recv()
        for copy in copies:
            copy.wait_send()

    deep, wide = z * 2 + c, x * Y + y

    def sum_of(buffer, count):
        total = buffer[0]
        for i in range(1, count):
            total = total + buffer[i]
        return total

    def merge(buffer, count):
        tiles = [buffer[i] for i in range(count)]
        total = sum(tiles[1:], tiles[0])
        mean = total[0:2, :] / jnp.maximum(total[4:5, :], 1.0)
        square = total[2:4, :]
        for tile in tiles:
            gap = tile[0:2, :] / jnp.maximum(tile[4:5, :], 1.0) - mean
            square = square + tile[4:5, :] * gap * gap
        return total[0:2, :], square, total[4:5, :]

    def write(buffer, place, sums, squares, number):
        buffer[place] = jnp.concatenate([sums, squares, number, jnp.zeros((3, 128), F32)], axis=0)

    number = jnp.sum(occ, axis=0, keepdims=True)
    sums = jnp.sum(conv, axis=0, keepdims=True)
    centred = (conv - sums / jnp.maximum(number, 1.0)) * occ
    squares = jnp.sum(centred * centred, axis=0, keepdims=True)
    write(deep1, deep, two(sums), two(squares), number[:, :128])
    copies = spread(deep1, deep, deep_group, d1_s, d1_r)
    conv_s[...] = conv
    for k in range(14):
        cols_t[k] = columns(k).T
    meet(copies, deep1, deep_group, d1_s, d1_r)
    write(wide1, wide, *merge(deep1, 2 * Z))
    copies = spread(wide1, wide, wide_group, w1_s, w1_r)
    for shift in range(2):
        gath_t[shift] = gath[shift].T
    meet(copies, wide1, wide_group, w1_s, w1_r)
    sums, squares, number = merge(wide1, X * Y)
    voxel_count = jnp.concatenate([number, number], axis=1)
    average = one(sums) / voxel_count
    inverse_std = lax.rsqrt(one(squares) / voxel_count + EPSILON)
    gamma, beta = gamma_ref[...], beta_ref[...]
    occ = occn[...]
    normalized = (conv_s[...] - average) * inverse_std
    normed = gamma * normalized + beta
    sigmoid = 1.0 / (1.0 + jnp.exp(-normed))
    act_grad = out_masked * sigmoid * (1.0 + normed * (1.0 - sigmoid))
    total = jnp.sum(act_grad, axis=0, keepdims=True)
    cross = jnp.sum(act_grad * normalized, axis=0, keepdims=True)
    write(deep2, deep, two(total), two(cross), jnp.zeros((1, 128), F32))
    copies = spread(deep2, deep, deep_group, d2_s, d2_r)
    centre = columns(13).astype(F32)
    block = (occ * (centre + normed * sigmoid)).astype(BF16)
    block_ref[...] = dot(to_bricks, block).astype(BF16).reshape(4, 64, 256)
    norm_s[...] = normalized
    for k in range(14, 27):
        cols_t[k] = columns(k).T
    meet(copies, deep2, deep_group, d2_s, d2_r)
    wide2[wide] = sum_of(deep2, 2 * Z)
    copies = spread(wide2, wide, wide_group, w2_s, w2_r)
    gath_t[2] = gath[2].T
    meet(copies, wide2, wide_group, w2_s, w2_r)
    tiles = sum_of(wide2, X * Y)
    total, cross = one(tiles[0:2]), one(tiles[2:4])
    inverse_root = lax.rsqrt(voxel_count)
    ggrad_ref[...] = cross * inverse_root
    bgrad_ref[...] = total * inverse_root
    conv_grad = (gamma * inverse_std * (act_grad - total / voxel_count - norm_s[...] * cross / voxel_count) * occ).astype(BF16)
    cg_s[...] = conv_grad

    mine = jnp.where(c == 0, conv_grad[:, :128].astype(F32), conv_grad[:, 128:].astype(F32)).astype(BF16)
    other = jnp.where(c == 0, conv_grad[:, 128:].astype(F32), conv_grad[:, :128].astype(F32)).astype(BF16)
    halves = jnp.concatenate([mine, other], axis=1)
    sister, here = device(z, x, y, 1 - c), device(z, x, y, c)
    small = 256 // (X * Y)
    half = pl.ds(pl.multiple_of(c * 128, 128), 128)
    other_half = pl.ds(pl.multiple_of((1 - c) * 128, 128), 128)
    depth = 8 // Z

    def axes(piece):
        return ((x, X), (y, Y)) if PIECES[piece][2] else ((y, Y), (x, X))

    def mate(piece, stage, step):
        if PIECES[piece][2] == (stage == 1):
            return device(z, ahead(x, step, X), y, c)
        return device(z, x, ahead(y, step, Y), c)

    def span(start, size):
        return pl.ds(pl.multiple_of(start, 16), size)

    def remote(source, target, send, receive, to):
        return pltpu.make_async_remote_copy(
            src_ref=source, dst_ref=target, send_sem=send, recv_sem=receive, device_id=to, device_id_type=MESH)

    going = {}
    sent = []

    def arrive(stage, piece):
        for copy in going.pop((stage, piece)):
            copy.wait()

    def heard(stage, piece):
        for copy in going.pop((stage, piece)):
            copy.wait_recv()

    def products(piece):
        first, count, _ = PIECES[piece]
        for k in range(first, first + count):
            product = dot(cols_t[k], halves)
            own[k] = product[:, :128]
            osend[k] = product[:, 128:].astype(BF16)
        copy = remote(osend.at[pl.ds(first, count)], crecv.at[pl.ds(first, count)], c_s.at[piece], c_r.at[piece], sister)
        copy.start()
        going["core", piece] = [copy]

    def stage1(piece):
        first, count, _ = PIECES[piece]
        (place, length), _ = axes(piece)
        rows = 256 // length
        arrive("core", piece)
        for k in range(first, first + count):
            value = own[k] + crecv[k].astype(F32)
            own[k] = value
            s1[k] = value.astype(BF16)
        going["one", piece] = []
        for step in range(1, length):
            copy = remote(
                s1.at[pl.ds(first, count), span(ahead(place, step, length) * rows, rows)],
                r1.at[step - 1, pl.ds(first, count)],
                q1_s.at[piece, step - 1], q1_r.at[piece, step - 1], mate(piece, 1, step))
            copy.start()
            going["one", piece].append(copy)

    def stage2(piece):
        first, count, _ = PIECES[piece]
        (place, length), (place2, length2) = axes(piece)
        rows = 256 // length
        arrive("one", piece)
        for k in range(first, first + count):
            value = own[k, span(place * rows, rows), :]
            for step in range(1, length):
                value = value + r1[step - 1, k].astype(F32)
            own[k, 0:rows, :] = value
            s2[k] = value.astype(BF16)
        going["two", piece] = []
        for step in range(1, length2):
            copy = remote(
                s2.at[pl.ds(first, count), span(ahead(place2, step, length2) * small, small)],
                r2.at[step - 1, pl.ds(first, count)],
                q2_s.at[piece, step - 1], q2_r.at[piece, step - 1], mate(piece, 2, step))
            copy.start()
            going["two", piece].append(copy)

    def stage3(piece):
        first, count, _ = PIECES[piece]
        _, (place2, length2) = axes(piece)
        arrive("two", piece)
        for k in range(8):
            if k < count:
                value = own[first + k, span(place2 * small, small), :]
                for step in range(1, length2):
                    value = value + r2[step - 1, first + k].astype(F32)
            else:
                value = jnp.zeros((small, 128), F32)
            s3[piece, k] = value
        going["three", piece] = []
        for dz in range(1, Z):
            copy = remote(
                s3.at[piece, pl.ds(ahead(z, dz, Z) * depth, depth)], r3.at[piece, dz - 1],
                q3_s.at[piece, dz - 1], q3_r.at[piece, dz - 1], device(ahead(z, dz, Z), x, y, c))
            copy.start()
            going["three", piece].append(copy)

    def fine(piece):
        (place, length), (place2, _) = axes(piece)
        return span(place * (256 // length) + place2 * small, small)

    def push(where, send, receive, to):
        return remote(outb.at[where], outb.at[where], send, receive, to)

    def back3(piece):
        arrive("three", piece)
        value = s3[piece, pl.ds(z * depth, depth)]
        for dz in range(1, Z):
            value = value + r3[piece, dz - 1]
        where = (pl.ds(piece * 8 + z * depth, depth), fine(piece), half)
        outb[where] = (value * inverse_root[:, :128].reshape(1, 1, 128)).astype(BF16)
        going["back3", piece] = []
        for dz in range(1, Z):
            copy = push(where, a3_s.at[piece, dz - 1], a3_r.at[piece, dz - 1], device(ahead(z, dz, Z), x, y, c))
            copy.start()
            sent.append(copy)
            going["back3", piece].append(push(
                (pl.ds(piece * 8 + ahead(z, -dz, Z) * depth, depth), fine(piece), half), a3_s.at[piece, dz - 1],
                a3_r.at[piece, dz - 1], here))

    def back2(piece):
        _, count, _ = PIECES[piece]
        (place, length), (place2, length2) = axes(piece)
        heard("back3", piece)
        going["back2", piece] = []
        for step in range(1, length2):
            copy = push((pl.ds(piece * 8, count), fine(piece), half), a2_s.at[piece, step - 1], a2_r.at[piece, step - 1],
                        mate(piece, 2, step))
            copy.start()
            sent.append(copy)
            start = place * (256 // length) + ahead(place2, -step, length2) * small
            going["back2", piece].append(push(
                (pl.ds(piece * 8, count), span(start, small), half), a2_s.at[piece, step - 1], a2_r.at[piece, step - 1],
                here))

    def back1(piece):
        _, count, _ = PIECES[piece]
        (place, length), _ = axes(piece)
        rows = 256 // length
        heard("back2", piece)
        going["back1", piece] = []
        for step in range(1, length):
            copy = push((pl.ds(piece * 8, count), span(place * rows, rows), half), a1_s.at[piece, step - 1],
                        a1_r.at[piece, step - 1], mate(piece, 1, step))
            copy.start()
            sent.append(copy)
            going["back1", piece].append(push(
                (pl.ds(piece * 8, count), span(ahead(place, -step, length) * rows, rows), half),
                a1_s.at[piece, step - 1], a1_r.at[piece, step - 1], here))

    def back0(piece):
        _, count, _ = PIECES[piece]
        heard("back1", piece)
        copy = push((pl.ds(piece * 8, count), pl.ds(0, 256), half), a0_s.at[piece], a0_r.at[piece], sister)
        copy.start()
        sent.append(copy)
        going["back0", piece] = [
            push((pl.ds(piece * 8, count), pl.ds(0, 256), other_half), a0_s.at[piece], a0_r.at[piece], here)]

    def finish(piece):
        heard("back0", piece)

    def column_grads():
        grad_s[...] = jnp.zeros_like(grad_s)
        for k in range(27):
            a, b, shift = k // 9, k // 3 % 3, k % 3
            product = lax.dot_general(cg_s[...], weight[k], (((1,), (1,)), ((), ())), preferred_element_type=F32)
            for i in range(4):
                start = (a + i) * 96 + b * 16
                grad_s[shift, start : start + 64, :] += product[i * 64 : (i + 1) * 64, :]

    def brick_grads():
        result = None
        for shift in range(3):
            value = grad_s[shift]
            high = value.astype(BF16)
            low = (value - high.astype(F32)).astype(BF16)
            term = dot(gath_t[shift], jnp.concatenate([high, low], axis=1))
            result = term if result is None else result + term
        result = result[:, :256] + result[:, 256:]
        local_s[...] = result[:256]
        ghosts[...] = result[256:].astype(BF16).reshape(8, 64, 256)
        going["ghosts", 0] = []
        for d in range(8):
            copy = remote(ghosts.at[d], returned.at[d], gh_s.at[d], gh_r.at[d], neighbour(-ROWS[d], -COLUMNS[d]))
            copy.start()
            going["ghosts", 0].append(copy)

    def feature_grads():
        out_bricks = dot(to_bricks, out_masked.astype(BF16))
        arrive("ghosts", 0)
        for b in range(4):
            rows = slice(b * 64, (b + 1) * 64)
            extra = out_bricks[rows] + local_s[rows, :]
            for d in range(8):
                extra = extra + jnp.where(send_ref[0, d] == b, returned[d].astype(F32), 0.0)
            fgrad_ref[b] = (extra * occ_brick[rows]).astype(BF16)

    schedule = (
        (products, 0), (products, 1), (products, 2), (products, 3),
        (stage1, 0), (stage1, 1), (stage1, 2), (stage1, 3),
        (column_grads,), (brick_grads,),
        (stage2, 0), (stage2, 1),
        (stage2, 2), (stage2, 3),
        (stage3, 0), (stage3, 1),
        (feature_grads,),
        (stage3, 2), (stage3, 3),
        (back3, 0), (back3, 1),
        (back3, 2), (back3, 3),
        (back2, 0), (back2, 1),
        (back2, 2), (back2, 3),
        (back1, 0), (back1, 1),
        (back1, 2), (back1, 3),
        (back0, 0), (back0, 1), (back0, 2), (back0, 3),
        (finish, 0), (finish, 1), (finish, 2), (finish, 3),
    )
    for step, *piece in schedule:
        step(*piece)
    for copy in sent:
        copy.wait_send()


def write_out(block, fgrad, wgrad, ggrad, bgrad, block_out, fgrad_out, wgrad_out, ggrad_out, bgrad_out, sems):
    pairs = [(block, block_out), (fgrad, fgrad_out), (ggrad, ggrad_out), (bgrad, bgrad_out)]
    for piece, (first, count, _) in enumerate(PIECES):
        pairs.append((wgrad.at[pl.ds(piece * 8, count)], wgrad_out.at[pl.ds(first, count)]))
    copies = [pltpu.make_async_copy(source, target, sems.at[i]) for i, (source, target) in enumerate(pairs)]
    for copy in copies:
        copy.start()
    for copy in copies:
        copy.wait()


def on_device(features, occupancy, neighbours, send_list, weight, gamma, beta, out_grad):
    vmem = pl.BlockSpec(memory_space=pltpu.VMEM)
    small = 256 // (X * Y)
    near, far = max(X, Y) - 1, Z - 1
    depth = 8 // Z
    pieces = len(PIECES)
    dma = pltpu.SemaphoreType.DMA
    scratch = [
        pltpu.VMEM((4, 64), I32),
        pltpu.VMEM((4, 27), I32),
        pltpu.VMEM((4, 64, 256), BF16),
        pltpu.VMEM((1, 256), F32),
        pltpu.VMEM((1, 256), F32),
        pltpu.VMEM((4, 64, 256), BF16),
        pltpu.VMEM((16, 128), F32),
        pltpu.VMEM((256, 256), F32),
        pltpu.VMEM((4, 64, 256), BF16),
        pltpu.VMEM((8, 64, 256), BF16),
        pltpu.VMEM((12, 64, 256), BF16),
        pltpu.VMEM((3, 576, 768), BF16),
        pltpu.VMEM((3, 768, 576), BF16),
        pltpu.VMEM((3, 576, 256), BF16),
        pltpu.VMEM((27, 256, 256), BF16),
        pltpu.VMEM((256, 256), F32),
        pltpu.VMEM((256, 256), F32),
        pltpu.VMEM((27, 256, 256), BF16),
        pltpu.VMEM((2 * Z, 8, 128), F32),
        pltpu.VMEM((X * Y, 8, 128), F32),
        pltpu.VMEM((2 * Z, 8, 128), F32),
        pltpu.VMEM((X * Y, 8, 128), F32),
        pltpu.VMEM((256, 256), BF16),
        pltpu.VMEM((3, 576, 256), F32),
        pltpu.VMEM((256, 256), F32),
        pltpu.VMEM((8, 64, 256), BF16),
        pltpu.VMEM((8, 64, 256), BF16),
        pltpu.VMEM((27, 256, 128), F32),
        pltpu.VMEM((27, 256, 128), BF16),
        pltpu.VMEM((27, 256, 128), BF16),
        pltpu.VMEM((27, 256, 128), BF16),
        pltpu.VMEM((near, 27, 256 // min(X, Y), 128), BF16),
        pltpu.VMEM((27, 256 // min(X, Y), 128), BF16),
        pltpu.VMEM((near, 27, small, 128), BF16),
        pltpu.VMEM((pieces, 8, small, 128), F32),
        pltpu.VMEM((pieces, far, depth, small, 128), F32),
        dma((7,)), dma((8,)), dma((8,)),
        dma((2 * Z - 1,)), dma((2 * Z - 1,)), dma((X * Y - 1,)), dma((X * Y - 1,)),
        dma((2 * Z - 1,)), dma((2 * Z - 1,)), dma((X * Y - 1,)), dma((X * Y - 1,)),
        dma((8,)), dma((8,)), dma((pieces,)), dma((pieces,)),
        dma((pieces, near)), dma((pieces, near)), dma((pieces, near)), dma((pieces, near)),
        dma((pieces, far)), dma((pieces, far)),
        dma((pieces, far)), dma((pieces, far)), dma((pieces, near)), dma((pieces, near)),
        dma((pieces, near)), dma((pieces, near)), dma((pieces,)), dma((pieces,)),
    ]
    anywhere = pl.BlockSpec(memory_space=pl.ANY)
    results = pl.pallas_call(
        kernel,
        name="brick_block",
        out_shape=(
            pltpu.VMEM((4, 64, 256), BF16),
            pltpu.VMEM((4, 64, 256), BF16),
            pltpu.VMEM((32, 256, 256), BF16),
            pltpu.VMEM((1, 256), F32),
            pltpu.VMEM((1, 256), F32),
        ),
        in_specs=[anywhere, anywhere, pl.BlockSpec(memory_space=pltpu.SMEM)] + [anywhere] * 5,
        out_specs=(vmem, vmem, vmem, vmem, vmem),
        scratch_shapes=scratch,
        compiler_params=pltpu.CompilerParams(
            collective_id=0, has_side_effects=True, vmem_limit_bytes=56 * 2**20),
    )(occupancy, neighbours, send_list.reshape(1, 8), features, gamma.reshape(1, 256), beta.reshape(1, 256), out_grad, weight)
    block, fgrad, wgrad, ggrad, bgrad = pl.pallas_call(
        write_out,
        name="write_out",
        out_shape=(
            jax.ShapeDtypeStruct((4, 64, 256), BF16),
            jax.ShapeDtypeStruct((4, 64, 256), BF16),
            jax.ShapeDtypeStruct((27, 256, 256), BF16),
            jax.ShapeDtypeStruct((1, 256), F32),
            jax.ShapeDtypeStruct((1, 256), F32),
        ),
        in_specs=[anywhere] * 5,
        out_specs=(anywhere,) * 5,
        scratch_shapes=[dma((4 + pieces,))],
        compiler_params=pltpu.CompilerParams(vmem_limit_bytes=8 * 2**20),
    )(*results)
    return block, fgrad, wgrad, ggrad.reshape(256), bgrad.reshape(256)


def solution(mesh):
    placed = (
        P(("gx", "gy"), None, None),
        P(("gx", "gy"), None),
        P(("gx", "gy"), None),
        P(("gx", "gy"), None, None),
        P(),
        P(),
        P(),
        P(("gx", "gy"), None, None),
    )
    return jax.shard_map(
        on_device,
        mesh=mesh,
        in_specs=placed,
        out_specs=(P(("gx", "gy"), None, None), P(("gx", "gy"), None, None), P(), P(), P()),
        check_vma=False,
    )
```

time: 114 us -> 96.3 us (0.84)
  Pallas kernels: 105 us -> 95.6 us
  local copies, waits for them, and re-layouts: 8.44 us -> 0 us
    pallas_call x1 -> x2, Pallas kernels: 105 us -> 95.6 us  [the longest x1 93.6 us: on_device(): pl.pallas_call(kernel, name='brick_block', out_shape=(pltpu.VMEM((4, 64,...]
    unnamed x9 -> x0, local copies, waits for them, and re-layouts: 8.44 us -> none
where the time goes in v2:
time: 96.3 us; the launch traced here: 96.2 us
  Pallas kernels  95.6 us (99%)
    pallas_call x1, Pallas kernels, on_device(): pl.pallas_call(kernel, name='brick_block', out_shape=(pltpu.VMEM((4, 64,...  93.6 us
    pallas_call x1, Pallas kernels, on_device(): pl.pallas_call(write_out, name='write_out', out_shape=(jax.ShapeDtypeStru...  1.95 us

profile of v2, /device:TPU:1, one launch (start us, length us, event | category | flops | bytes accessed | tf_op | source)
XLA Modules:
  0.0 96.2 jit_solution(16467610029727830669)
XLA Ops:
  0.6 93.6 %brick_block.1 = (bf16[4,64,256]{2,1,0:T(8,128)(2,1)S(1)}, bf16[4,64,256]{2,1,0:T(8,128)(2,1)S(1)}, bf16[32,256,256]{2,1,0:T(8,128)(2,1)S(1)}, f32[1,256]{1,0:T(1,128)S(1)}, f32[1,256]{1,0:T(1,128)S(1)}) custom-call(s32[4,64]{1,0:T(4,128)} %occ_hbm.1, s32[4,27]{1,0:T(4,128)} %nb_hbm.1, s32[1,8]{1,0:T(1,128)} %bitcast.7, bf16[4,64,256]{2,1,0:T(8,128)(2,1)} %feat_hbm.1, ...), custom_call_target="tpu_custom_call" | custom-call | tf_op jit(solution)/shard_map/brick_block/pallas_call | solution.py:561
  94.3 2.0 %write_out.1 = (bf16[4,64,256]{2,1,0:T(8,128)(2,1)}, bf16[4,64,256]{2,1,0:T(8,128)(2,1)}, bf16[27,256,256]{2,1,0:T(8,128)(2,1)}, f32[1,256]{1,0:T(1,128)}, f32[1,256]{1,0:T(1,128)}) custom-call(bf16[4,64,256]{2,1,0:T(8,128)(2,1)S(1)} %get-tuple-element.15.block, bf16[4,64,256]{2,1,0:T(8,128)(2,1)S(1)} %get-tuple-element.16.fgrad, ...), custom_call_target="tpu_custom_call" | custom-call | tf_op jit(solution)/shard_map/write_out/pallas_call | solution.py:577

commit v3 on v2

--- a/solution.py
+++ b/solution.py
@@ -16,7 +16,12 @@
 MESH = pl.DeviceIdType.MESH
 F32, BF16, I32 = jnp.float32, jnp.bfloat16, jnp.int32
 
-PIECES = ((0, 8, True), (8, 8, False), (16, 6, True), (22, 5, False))
+PARTS = ((0, 14), (14, 13))
+PIECES = ((0, 6, 0), (14, 6, 1), (6, 8, 0), (20, 7, 1))
+
+
+def far_first(count):
+    return sorted(range(1, count), key=lambda step: -min(step, count - step))
 
 
 def coordinates():
@@ -49,9 +54,9 @@
     occ_ref, nb_ref, feat_ref, gamma_ref, beta_ref, og_ref, tab, occn, masked, packets, ext, gath, gath_t, slabs, weight, conv_s, norm_s, cols_t,
     deep1, wide1, deep2, wide2,
     cg_s, grad_s, local_s, ghosts, returned,
-    own, osend, crecv, s1, r1, s2, r2, s3, r3,
+    cols_sister, half_grads, own, s1, r1, s2, r2, s3, t3, r3, gathered,
     in_sem, halo_s, halo_r, d1_s, d1_r, w1_s, w1_r, d2_s, d2_r, w2_s, w2_r,
-    gh_s, gh_r, c_s, c_r, q1_s, q1_r, q2_s, q2_r, q3_s, q3_r, a3_s, a3_r, a2_s, a2_r, a1_s, a1_r, a0_s, a0_r,
+    gh_s, gh_r, cols_s, cols_r, c_s, c_r, q1_s, q1_r, q2_s, q2_r, q3_s, q3_r, a3_s, a3_r, a2_s, a2_r, a1_s, a1_r, a0_s, a0_r,
 ):
     z, x, y, c = coordinates()
     gx, gy = lax.axis_index("gx"), lax.axis_index("gy")
@@ -62,24 +67,35 @@
 
     deep_group = [
         (device(ahead(z, dz, Z), x, y, ahead(c, dc, 2)), ahead(z, -dz, Z) * 2 + ahead(c, dc, 2))
-        for dz in range(Z) for dc in range(2) if dz + dc > 0]
+        for dz in far_first(Z) + [0] for dc in (1, 0) if dz + dc > 0]
     wide_group = [
         (device(z, ahead(x, dx, X), ahead(y, dy, Y), c), ahead(x, -dx, X) * Y + ahead(y, -dy, Y))
-        for dx in range(X) for dy in range(Y) if dx + dy > 0]
+        for dx, dy in sorted(
+            ((dx, dy) for dx in range(X) for dy in range(Y) if dx + dy > 0),
+            key=lambda step: -min(step[0], X - step[0]) - min(step[1], Y - step[1]))]
+
+    inputs = [
+        pltpu.make_async_copy(source, target, in_sem.at[i])
+        for i, (source, target) in enumerate((
+            (occ_hbm, occ_ref), (feat_hbm, feat_ref), (nb_hbm, nb_ref), (og_hbm, og_ref),
+            (gamma_hbm, gamma_ref), (beta_hbm, beta_ref), (w_hbm, weight)))]
+    inputs[0].start()
+    inputs[1].start()
 
     barrier = pltpu.get_barrier_semaphore()
     friends = [neighbour(ROWS[d], COLUMNS[d]) for d in range(8)]
     friends += [friend for friend, _ in deep_group + wide_group]
     for friend in friends:
         pl.semaphore_signal(barrier, inc=1, device_id=friend, device_id_type=MESH)
-
-    inputs = [
-        pltpu.make_async_copy(source, target, in_sem.at[i])
-        for i, (source, target) in enumerate((
-            (occ_hbm, occ_ref), (feat_hbm, feat_ref), (nb_hbm, nb_ref), (og_hbm, og_ref),
-            (gamma_hbm, gamma_ref), (beta_hbm, beta_ref), (w_hbm, weight)))]
-    for copy in inputs:
+    for copy in inputs[2:]:
         copy.start()
+
+    sent = []
+
+    def settle():
+        for copy in sent:
+            copy.wait_send()
+        sent.clear()
 
     tab[...] = jnp.zeros_like(tab)
     inputs[0].wait()
@@ -156,7 +172,8 @@
             gath[shift, :, j * 128 : (j + 1) * 128] = jnp.where(source == lane_f + 128.0 * j, 1.0, 0.0).astype(BF16)
 
     for copy in halo:
-        copy.wait()
+        copy.wait_recv()
+    sent.extend(halo)
     extended = ext[...].reshape(768, 256)
     for shift in range(3):
         slabs[shift] = dot(gath[shift], extended).astype(BF16)
@@ -193,8 +210,7 @@
             pltpu.make_async_remote_copy(
                 src_ref=buffer.at[behind], dst_ref=buffer.at[behind], send_sem=send.at[i], recv_sem=receive.at[i],
                 device_id=friend, device_id_type=MESH).wait_recv()
-        for copy in copies:
-            copy.wait_send()
+        sent.extend(copies)
 
     deep, wide = z * 2 + c, x * Y + y
 
@@ -224,8 +240,18 @@
     write(deep1, deep, two(sums), two(squares), number[:, :128])
     copies = spread(deep1, deep, deep_group, d1_s, d1_r)
     conv_s[...] = conv
-    for k in range(14):
-        cols_t[k] = columns(k).T
+    sister, here = device(z, x, y, 1 - c), device(z, x, y, c)
+
+    def share_columns(first, count, i):
+        for k in range(first, first + count):
+            cols_t[k] = columns(k).T
+        copy = pltpu.make_async_remote_copy(
+            src_ref=cols_t.at[pl.ds(first, count)], dst_ref=cols_sister.at[pl.ds(first, count)],
+            send_sem=cols_s.at[i], recv_sem=cols_r.at[i], device_id=sister, device_id_type=MESH)
+        copy.start()
+        return copy
+
+    shared = [share_columns(0, 14, 0)]
     meet(copies, deep1, deep_group, d1_s, d1_r)
     write(wide1, wide, *merge(deep1, 2 * Z))
     copies = spread(wide1, wide, wide_group, w1_s, w1_r)
@@ -250,8 +276,7 @@
     block = (occ * (centre + normed * sigmoid)).astype(BF16)
     block_ref[...] = dot(to_bricks, block).astype(BF16).reshape(4, 64, 256)
     norm_s[...] = normalized
-    for k in range(14, 27):
-        cols_t[k] = columns(k).T
+    shared.append(share_columns(14, 13, 1))
     meet(copies, deep2, deep_group, d2_s, d2_r)
     wide2[wide] = sum_of(deep2, 2 * Z)
     copies = spread(wide2, wide, wide_group, w2_s, w2_r)
@@ -265,20 +290,22 @@
     conv_grad = (gamma * inverse_std * (act_grad - total / voxel_count - norm_s[...] * cross / voxel_count) * occ).astype(BF16)
     cg_s[...] = conv_grad
 
-    mine = jnp.where(c == 0, conv_grad[:, :128].astype(F32), conv_grad[:, 128:].astype(F32)).astype(BF16)
-    other = jnp.where(c == 0, conv_grad[:, 128:].astype(F32), conv_grad[:, :128].astype(F32)).astype(BF16)
-    halves = jnp.concatenate([mine, other], axis=1)
-    sister, here = device(z, x, y, 1 - c), device(z, x, y, c)
+    half_grads[0] = jnp.where(c == 0, conv_grad[:, :128].astype(F32), conv_grad[:, 128:].astype(F32)).astype(BF16)
+    half_grads[1] = jnp.where(c == 0, conv_grad[:, 128:].astype(F32), conv_grad[:, :128].astype(F32)).astype(BF16)
+    shared.append(pltpu.make_async_remote_copy(
+        src_ref=half_grads.at[1], dst_ref=half_grads.at[2], send_sem=c_s, recv_sem=c_r,
+        device_id=sister, device_id_type=MESH))
+    shared[2].start()
     small = 256 // (X * Y)
     half = pl.ds(pl.multiple_of(c * 128, 128), 128)
     other_half = pl.ds(pl.multiple_of((1 - c) * 128, 128), 128)
-    depth = 8 // Z
-
-    def axes(piece):
-        return ((x, X), (y, Y)) if PIECES[piece][2] else ((y, Y), (x, X))
-
-    def mate(piece, stage, step):
-        if PIECES[piece][2] == (stage == 1):
+    depth = 16 // Z
+
+    def axes(part):
+        return ((y, Y), (x, X)) if part else ((x, X), (y, Y))
+
+    def mate(part, stage, step):
+        if part == stage - 1:
             return device(z, ahead(x, step, X), y, c)
         return device(z, x, ahead(y, step, Y), c)
 
@@ -290,11 +317,11 @@
             src_ref=source, dst_ref=target, send_sem=send, recv_sem=receive, device_id=to, device_id_type=MESH)
 
     going = {}
-    sent = []
 
     def arrive(stage, piece):
         for copy in going.pop((stage, piece)):
-            copy.wait()
+            copy.wait_recv()
+            sent.append(copy)
 
     def heard(stage, piece):
         for copy in going.pop((stage, piece)):
@@ -303,135 +330,141 @@
     def products(piece):
         first, count, _ = PIECES[piece]
         for k in range(first, first + count):
-            product = dot(cols_t[k], halves)
-            own[k] = product[:, :128]
-            osend[k] = product[:, 128:].astype(BF16)
-        copy = remote(osend.at[pl.ds(first, count)], crecv.at[pl.ds(first, count)], c_s.at[piece], c_r.at[piece], sister)
-        copy.start()
-        going["core", piece] = [copy]
+            own[k] = dot(cols_t[k], half_grads[0])
+
+    def hear_sister():
+        for copy in shared:
+            copy.wait_recv()
+            sent.append(copy)
 
     def stage1(piece):
-        first, count, _ = PIECES[piece]
-        (place, length), _ = axes(piece)
+        first, count, part = PIECES[piece]
+        (place, length), _ = axes(part)
         rows = 256 // length
-        arrive("core", piece)
         for k in range(first, first + count):
-            value = own[k] + crecv[k].astype(F32)
+            value = own[k] + dot(cols_sister[k], half_grads[2])
             own[k] = value
             s1[k] = value.astype(BF16)
-        going["one", piece] = []
-        for step in range(1, length):
+        for step in far_first(length):
             copy = remote(
                 s1.at[pl.ds(first, count), span(ahead(place, step, length) * rows, rows)],
                 r1.at[step - 1, pl.ds(first, count)],
-                q1_s.at[piece, step - 1], q1_r.at[piece, step - 1], mate(piece, 1, step))
+                q1_s.at[piece, step - 1], q1_r.at[piece, step - 1], mate(part, 1, step))
             copy.start()
-            going["one", piece].append(copy)
-
-    def stage2(piece):
-        first, count, _ = PIECES[piece]
-        (place, length), (place2, length2) = axes(piece)
+            going.setdefault(("one", part), []).append(copy)
+
+    def stage2(part):
+        first, count = PARTS[part]
+        (place, length), (place2, length2) = axes(part)
         rows = 256 // length
-        arrive("one", piece)
+        arrive("one", part)
         for k in range(first, first + count):
             value = own[k, span(place * rows, rows), :]
             for step in range(1, length):
                 value = value + r1[step - 1, k].astype(F32)
             own[k, 0:rows, :] = value
             s2[k] = value.astype(BF16)
-        going["two", piece] = []
-        for step in range(1, length2):
+        going["two", part] = []
+        for step in far_first(length2):
             copy = remote(
                 s2.at[pl.ds(first, count), span(ahead(place2, step, length2) * small, small)],
                 r2.at[step - 1, pl.ds(first, count)],
-                q2_s.at[piece, step - 1], q2_r.at[piece, step - 1], mate(piece, 2, step))
+                q2_s.at[part, step - 1], q2_r.at[part, step - 1], mate(part, 2, step))
             copy.start()
-            going["two", piece].append(copy)
-
-    def stage3(piece):
-        first, count, _ = PIECES[piece]
-        _, (place2, length2) = axes(piece)
-        arrive("two", piece)
-        for k in range(8):
-            if k < count:
-                value = own[first + k, span(place2 * small, small), :]
-                for step in range(1, length2):
-                    value = value + r2[step - 1, first + k].astype(F32)
-            else:
-                value = jnp.zeros((small, 128), F32)
-            s3[piece, k] = value
-        going["three", piece] = []
-        for dz in range(1, Z):
+            going["two", part].append(copy)
+
+    def stage3():
+        for part, (first, count) in enumerate(PARTS):
+            _, (place2, length2) = axes(part)
+            arrive("two", part)
+            for k in range(16):
+                if k < count:
+                    value = own[first + k, span(place2 * small, small), :]
+                    for step in range(1, length2):
+                        value = value + r2[step - 1, first + k].astype(F32)
+                else:
+                    value = jnp.zeros((small, 128), F32)
+                t3[k, part] = value
+                s3[k, part] = value.astype(BF16)
+        going["three", 0] = []
+        for dz in far_first(Z):
             copy = remote(
-                s3.at[piece, pl.ds(ahead(z, dz, Z) * depth, depth)], r3.at[piece, dz - 1],
-                q3_s.at[piece, dz - 1], q3_r.at[piece, dz - 1], device(ahead(z, dz, Z), x, y, c))
+                s3.at[pl.ds(ahead(z, dz, Z) * depth, depth)], r3.at[dz - 1],
+                q3_s.at[dz - 1], q3_r.at[dz - 1], device(ahead(z, dz, Z), x, y, c))
             copy.start()
-            going["three", piece].append(copy)
-
-    def fine(piece):
-        (place, length), (place2, _) = axes(piece)
+            going["three", 0].append(copy)
+
+    def fine(part):
+        (place, length), (place2, _) = axes(part)
         return span(place * (256 // length) + place2 * small, small)
 
     def push(where, send, receive, to):
         return remote(outb.at[where], outb.at[where], send, receive, to)
 
-    def back3(piece):
-        arrive("three", piece)
-        value = s3[piece, pl.ds(z * depth, depth)]
+    def back3():
+        arrive("three", 0)
+        mine = pl.ds(z * depth, depth)
+        value = t3[mine]
         for dz in range(1, Z):
-            value = value + r3[piece, dz - 1]
-        where = (pl.ds(piece * 8 + z * depth, depth), fine(piece), half)
-        outb[where] = (value * inverse_root[:, :128].reshape(1, 1, 128)).astype(BF16)
-        going["back3", piece] = []
-        for dz in range(1, Z):
-            copy = push(where, a3_s.at[piece, dz - 1], a3_r.at[piece, dz - 1], device(ahead(z, dz, Z), x, y, c))
+            value = value + r3[dz - 1].astype(F32)
+        gathered[mine] = (value * inverse_root[:, :128].reshape(1, 1, 1, 128)).astype(BF16)
+        going["back3", 0] = []
+        for dz in far_first(Z):
+            copy = remote(gathered.at[mine], gathered.at[mine], a3_s.at[dz - 1], a3_r.at[dz - 1],
+                          device(ahead(z, dz, Z), x, y, c))
             copy.start()
             sent.append(copy)
-            going["back3", piece].append(push(
-                (pl.ds(piece * 8 + ahead(z, -dz, Z) * depth, depth), fine(piece), half), a3_s.at[piece, dz - 1],
-                a3_r.at[piece, dz - 1], here))
-
-    def back2(piece):
-        _, count, _ = PIECES[piece]
-        (place, length), (place2, length2) = axes(piece)
-        heard("back3", piece)
-        going["back2", piece] = []
-        for step in range(1, length2):
-            copy = push((pl.ds(piece * 8, count), fine(piece), half), a2_s.at[piece, step - 1], a2_r.at[piece, step - 1],
-                        mate(piece, 2, step))
+            behind = gathered.at[pl.ds(ahead(z, -dz, Z) * depth, depth)]
+            going["back3", 0].append(remote(behind, behind, a3_s.at[dz - 1], a3_r.at[dz - 1], here))
+
+    def back2():
+        heard("back3", 0)
+        for part, (_, count) in enumerate(PARTS):
+            (place, length), (place2, length2) = axes(part)
+            going["back2", part] = []
+            for step in far_first(length2):
+                copy = remote(gathered.at[pl.ds(0, count), part], outb.at[pl.ds(part * 16, count), fine(part), half],
+                              a2_s.at[part, step - 1], a2_r.at[part, step - 1], mate(part, 2, step))
+                copy.start()
+                sent.append(copy)
+                start = place * (256 // length) + ahead(place2, -step, length2) * small
+                going["back2", part].append(push(
+                    (pl.ds(part * 16, count), span(start, small), half), a2_s.at[part, step - 1],
+                    a2_r.at[part, step - 1], here))
+        for part, (_, count) in enumerate(PARTS):
+            outb[pl.ds(part * 16, count), fine(part), half] = gathered[0:count, part]
+
+    def strip(part, step, lanes):
+        (place, length), _ = axes(part)
+        rows = 256 // length
+        return pl.ds(part * 16, PARTS[part][1]), span(ahead(place, -step, length) * rows, rows), lanes
+
+    def hand_over(part, step):
+        copy = push(strip(part, step, half), a0_s.at[part, step], a0_r.at[part, step], sister)
+        copy.start()
+        sent.append(copy)
+
+    def back1(part):
+        _, length = axes(part)[0]
+        heard("back2", part)
+        for step in far_first(length):
+            copy = push(strip(part, 0, half), a1_s.at[part, step - 1], a1_r.at[part, step - 1], mate(part, 1, step))
             copy.start()
             sent.append(copy)
-            start = place * (256 // length) + ahead(place2, -step, length2) * small
-            going["back2", piece].append(push(
-                (pl.ds(piece * 8, count), span(start, small), half), a2_s.at[piece, step - 1], a2_r.at[piece, step - 1],
-                here))
-
-    def back1(piece):
-        _, count, _ = PIECES[piece]
-        (place, length), _ = axes(piece)
-        rows = 256 // length
-        heard("back2", piece)
-        going["back1", piece] = []
-        for step in range(1, length):
-            copy = push((pl.ds(piece * 8, count), span(place * rows, rows), half), a1_s.at[piece, step - 1],
-                        a1_r.at[piece, step - 1], mate(piece, 1, step))
-            copy.start()
-            sent.append(copy)
-            going["back1", piece].append(push(
-                (pl.ds(piece * 8, count), span(ahead(place, -step, length) * rows, rows), half),
-                a1_s.at[piece, step - 1], a1_r.at[piece, step - 1], here))
-
-    def back0(piece):
-        _, count, _ = PIECES[piece]
-        heard("back1", piece)
-        copy = push((pl.ds(piece * 8, count), pl.ds(0, 256), half), a0_s.at[piece], a0_r.at[piece], sister)
-        copy.start()
-        sent.append(copy)
-        going["back0", piece] = [
-            push((pl.ds(piece * 8, count), pl.ds(0, 256), other_half), a0_s.at[piece], a0_r.at[piece], here)]
-
-    def finish(piece):
-        heard("back0", piece)
+        hand_over(part, 0)
+
+    def back0():
+        for step in (1, 3, 2):
+            for part in range(2):
+                if step < axes(part)[0][1]:
+                    push(strip(part, step, half), a1_s.at[part, step - 1], a1_r.at[part, step - 1], here).wait_recv()
+                    hand_over(part, step)
+
+    def finish():
+        for step in (0, 1, 3, 2):
+            for part in range(2):
+                if step < axes(part)[0][1]:
+                    push(strip(part, step, other_half), a0_s.at[part, step], a0_r.at[part, step], here).wait_recv()
 
     def column_grads():
         grad_s[...] = jnp.zeros_like(grad_s)
@@ -470,33 +503,26 @@
             fgrad_ref[b] = (extra * occ_brick[rows]).astype(BF16)
 
     schedule = (
-        (products, 0), (products, 1), (products, 2), (products, 3),
-        (stage1, 0), (stage1, 1), (stage1, 2), (stage1, 3),
-        (column_grads,), (brick_grads,),
-        (stage2, 0), (stage2, 1),
-        (stage2, 2), (stage2, 3),
-        (stage3, 0), (stage3, 1),
+        (products, 0), (products, 1), (hear_sister,),
+        (stage1, 0), (stage1, 1),
+        (products, 2), (products, 3), (stage1, 2), (stage1, 3),
+        (column_grads,), (settle,),
+        (stage2, 0), (stage2, 1), (stage3,),
+        (brick_grads,), (back3,),
         (feature_grads,),
-        (stage3, 2), (stage3, 3),
-        (back3, 0), (back3, 1),
-        (back3, 2), (back3, 3),
-        (back2, 0), (back2, 1),
-        (back2, 2), (back2, 3),
+        (back2,),
         (back1, 0), (back1, 1),
-        (back1, 2), (back1, 3),
-        (back0, 0), (back0, 1), (back0, 2), (back0, 3),
-        (finish, 0), (finish, 1), (finish, 2), (finish, 3),
+        (settle,),
+        (back0,), (finish,), (settle,),
     )
     for step, *piece in schedule:
         step(*piece)
-    for copy in sent:
-        copy.wait_send()
 
 
 def write_out(block, fgrad, wgrad, ggrad, bgrad, block_out, fgrad_out, wgrad_out, ggrad_out, bgrad_out, sems):
     pairs = [(block, block_out), (fgrad, fgrad_out), (ggrad, ggrad_out), (bgrad, bgrad_out)]
-    for piece, (first, count, _) in enumerate(PIECES):
-        pairs.append((wgrad.at[pl.ds(piece * 8, count)], wgrad_out.at[pl.ds(first, count)]))
+    for part, (first, count) in enumerate(PARTS):
+        pairs.append((wgrad.at[pl.ds(part * 16, count)], wgrad_out.at[pl.ds(first, count)]))
     copies = [pltpu.make_async_copy(source, target, sems.at[i]) for i, (source, target) in enumerate(pairs)]
     for copy in copies:
         copy.start()
@@ -508,7 +534,7 @@
     vmem = pl.BlockSpec(memory_space=pltpu.VMEM)
     small = 256 // (X * Y)
     near, far = max(X, Y) - 1, Z - 1
-    depth = 8 // Z
+    depth = 16 // Z
     pieces = len(PIECES)
     dma = pltpu.SemaphoreType.DMA
     scratch = [
@@ -539,23 +565,24 @@
         pltpu.VMEM((256, 256), F32),
         pltpu.VMEM((8, 64, 256), BF16),
         pltpu.VMEM((8, 64, 256), BF16),
+        pltpu.VMEM((27, 256, 256), BF16),
+        pltpu.VMEM((3, 256, 128), BF16),
         pltpu.VMEM((27, 256, 128), F32),
-        pltpu.VMEM((27, 256, 128), BF16),
-        pltpu.VMEM((27, 256, 128), BF16),
         pltpu.VMEM((27, 256, 128), BF16),
         pltpu.VMEM((near, 27, 256 // min(X, Y), 128), BF16),
         pltpu.VMEM((27, 256 // min(X, Y), 128), BF16),
         pltpu.VMEM((near, 27, small, 128), BF16),
-        pltpu.VMEM((pieces, 8, small, 128), F32),
-        pltpu.VMEM((pieces, far, depth, small, 128), F32),
+        pltpu.VMEM((16, 2, small, 128), BF16),
+        pltpu.VMEM((16, 2, small, 128), F32),
+        pltpu.VMEM((far, depth, 2, small, 128), BF16),
+        pltpu.VMEM((16, 2, small, 128), BF16),
         dma((7,)), dma((8,)), dma((8,)),
         dma((2 * Z - 1,)), dma((2 * Z - 1,)), dma((X * Y - 1,)), dma((X * Y - 1,)),
         dma((2 * Z - 1,)), dma((2 * Z - 1,)), dma((X * Y - 1,)), dma((X * Y - 1,)),
-        dma((8,)), dma((8,)), dma((pieces,)), dma((pieces,)),
-        dma((pieces, near)), dma((pieces, near)), dma((pieces, near)), dma((pieces, near)),
-        dma((pieces, far)), dma((pieces, far)),
-        dma((pieces, far)), dma((pieces, far)), dma((pieces, near)), dma((pieces, near)),
-        dma((pieces, near)), dma((pieces, near)), dma((pieces,)), dma((pieces,)),
+        dma((8,)), dma((8,)), dma((2,)), dma((2,)), dma, dma,
+        dma((pieces, near)), dma((pieces, near)), dma((2, near)), dma((2, near)), dma((far,)), dma((far,)),
+        dma((far,)), dma((far,)), dma((2, near)), dma((2, near)),
+        dma((2, near)), dma((2, near)), dma((2, near + 1)), dma((2, near + 1)),
     ]
     anywhere = pl.BlockSpec(memory_space=pl.ANY)
     results = pl.pallas_call(
@@ -586,7 +613,7 @@
         ),
         in_specs=[anywhere] * 5,
         out_specs=(anywhere,) * 5,
-        scratch_shapes=[dma((4 + pieces,))],
+        scratch_shapes=[dma((6,))],
         compiler_params=pltpu.CompilerParams(vmem_limit_bytes=8 * 2**20),
     )(*results)
     return block, fgrad, wgrad, ggrad.reshape(256), bgrad.reshape(256)

time: 96.3 us -> 94.5 us (0.981)
  Pallas kernels: 95.6 us -> 93.7 us
    pallas_call x1, Pallas kernels: 93.6 us -> 91.8 us  [on_device(): pl.pallas_call(kernel, name='brick_block', out_shape=(pltpu.VMEM((4, 64,...]
where the time goes in v3:
time: 94.5 us; the launch traced here: 94.4 us
  Pallas kernels  93.7 us (99%)
    pallas_call x1, Pallas kernels, on_device(): pl.pallas_call(kernel, name='brick_block', out_shape=(pltpu.VMEM((4, 64,...  91.8 us
    pallas_call x1, Pallas kernels, on_device(): pl.pallas_call(write_out, name='write_out', out_shape=(jax.ShapeDtypeStru...  1.94 us

profile of v3, /device:TPU:1, one launch (start us, length us, event | category | flops | bytes accessed | tf_op | source)
XLA Modules:
  0.0 94.4 jit_solution(7691213252195120421)
XLA Ops:
  0.6 91.8 %brick_block.1 = (bf16[4,64,256]{2,1,0:T(8,128)(2,1)S(1)}, bf16[4,64,256]{2,1,0:T(8,128)(2,1)S(1)}, bf16[32,256,256]{2,1,0:T(8,128)(2,1)S(1)}, f32[1,256]{1,0:T(1,128)S(1)}, f32[1,256]{1,0:T(1,128)S(1)}) custom-call(s32[4,64]{1,0:T(4,128)} %occ_hbm.1, s32[4,27]{1,0:T(4,128)} %nb_hbm.1, s32[1,8]{1,0:T(1,128)} %bitcast.7, bf16[4,64,256]{2,1,0:T(8,128)(2,1)} %feat_hbm.1, ...), custom_call_target="tpu_custom_call" | custom-call | tf_op jit(solution)/shard_map/brick_block/pallas_call | solution.py:588
  92.4 1.9 %write_out.1 = (bf16[4,64,256]{2,1,0:T(8,128)(2,1)}, bf16[4,64,256]{2,1,0:T(8,128)(2,1)}, bf16[27,256,256]{2,1,0:T(8,128)(2,1)}, f32[1,256]{1,0:T(1,128)}, f32[1,256]{1,0:T(1,128)}) custom-call(bf16[4,64,256]{2,1,0:T(8,128)(2,1)S(1)} %get-tuple-element.15.block, bf16[4,64,256]{2,1,0:T(8,128)(2,1)S(1)} %get-tuple-element.16.fgrad, ...), custom_call_target="tpu_custom_call" | custom-call | tf_op jit(solution)/shard_map/write_out/pallas_call | solution.py:604

commit v4 on v3

--- a/solution.py
+++ b/solution.py
@@ -16,8 +16,13 @@
 MESH = pl.DeviceIdType.MESH
 F32, BF16, I32 = jnp.float32, jnp.bfloat16, jnp.int32
 
-PARTS = ((0, 14), (14, 13))
-PIECES = ((0, 6, 0), (14, 6, 1), (6, 8, 0), (20, 7, 1))
+PARTS = ((0, 11), (11, 11))
+PIECES = ((0, 5, 0), (11, 5, 1), (5, 6, 0), (16, 6, 1))
+THIRD = (22, 5)
+
+
+def slots():
+    return -(-THIRD[0] // Z) * Z
 
 
 def far_first(count):
@@ -54,9 +59,10 @@
     occ_ref, nb_ref, feat_ref, gamma_ref, beta_ref, og_ref, tab, occn, masked, packets, ext, gath, gath_t, slabs, weight, conv_s, norm_s, cols_t,
     deep1, wide1, deep2, wide2,
     cg_s, grad_s, local_s, ghosts, returned,
-    cols_sister, half_grads, own, s1, r1, s2, r2, s3, t3, r3, gathered,
+    cols_sister, half_grads, own, s1, r1, s2, r2, s3, t3, r3, gathered, rz, own2z, s2z, r2z, own3z, s3z, r3z,
     in_sem, halo_s, halo_r, d1_s, d1_r, w1_s, w1_r, d2_s, d2_r, w2_s, w2_r,
     gh_s, gh_r, cols_s, cols_r, c_s, c_r, q1_s, q1_r, q2_s, q2_r, q3_s, q3_r, a3_s, a3_r, a2_s, a2_r, a1_s, a1_r, a0_s, a0_r,
+    z1_s, z1_r, z2_s, z2_r, z3_s, z3_r, b3_s, b3_r, b2_s, b2_r, b1_s, b1_r, b0_s, b0_r,
 ):
     z, x, y, c = coordinates()
     gx, gy = lax.axis_index("gx"), lax.axis_index("gy")
@@ -299,7 +305,11 @@
     small = 256 // (X * Y)
     half = pl.ds(pl.multiple_of(c * 128, 128), 128)
     other_half = pl.ds(pl.multiple_of((1 - c) * 128, 128), 128)
-    depth = 16 // Z
+    depth = slots() // Z
+    first_z, count_z = THIRD
+    owners = [i * Z // count_z for i in range(count_z)]
+    slot = sum(i * (z == owner).astype(I32) for i, owner in enumerate(owners))
+    is_owner = sum((z == owner).astype(I32) for owner in owners) > 0
 
     def axes(part):
         return ((y, Y), (x, X)) if part else ((x, X), (y, Y))
@@ -377,15 +387,15 @@
         for part, (first, count) in enumerate(PARTS):
             _, (place2, length2) = axes(part)
             arrive("two", part)
-            for k in range(16):
-                if k < count:
-                    value = own[first + k, span(place2 * small, small), :]
-                    for step in range(1, length2):
-                        value = value + r2[step - 1, first + k].astype(F32)
-                else:
-                    value = jnp.zeros((small, 128), F32)
-                t3[k, part] = value
-                s3[k, part] = value.astype(BF16)
+            for k in range(first, first + count):
+                value = own[k, span(place2 * small, small), :]
+                for step in range(1, length2):
+                    value = value + r2[step - 1, k].astype(F32)
+                t3[k] = value
+                s3[k] = value.astype(BF16)
+        for k in range(first_z, slots()):
+            t3[k] = jnp.zeros((small, 128), F32)
+            s3[k] = jnp.zeros((small, 128), BF16)
         going["three", 0] = []
         for dz in far_first(Z):
             copy = remote(
@@ -407,7 +417,7 @@
         value = t3[mine]
         for dz in range(1, Z):
             value = value + r3[dz - 1].astype(F32)
-        gathered[mine] = (value * inverse_root[:, :128].reshape(1, 1, 1, 128)).astype(BF16)
+        gathered[mine] = (value * inverse_root[:, :128].reshape(1, 1, 128)).astype(BF16)
         going["back3", 0] = []
         for dz in far_first(Z):
             copy = remote(gathered.at[mine], gathered.at[mine], a3_s.at[dz - 1], a3_r.at[dz - 1],
@@ -419,25 +429,25 @@
 
     def back2():
         heard("back3", 0)
-        for part, (_, count) in enumerate(PARTS):
+        for part, (first, count) in enumerate(PARTS):
             (place, length), (place2, length2) = axes(part)
             going["back2", part] = []
             for step in far_first(length2):
-                copy = remote(gathered.at[pl.ds(0, count), part], outb.at[pl.ds(part * 16, count), fine(part), half],
+                copy = remote(gathered.at[pl.ds(first, count)], outb.at[pl.ds(first, count), fine(part), half],
                               a2_s.at[part, step - 1], a2_r.at[part, step - 1], mate(part, 2, step))
                 copy.start()
                 sent.append(copy)
                 start = place * (256 // length) + ahead(place2, -step, length2) * small
                 going["back2", part].append(push(
-                    (pl.ds(part * 16, count), span(start, small), half), a2_s.at[part, step - 1],
+                    (pl.ds(first, count), span(start, small), half), a2_s.at[part, step - 1],
                     a2_r.at[part, step - 1], here))
-        for part, (_, count) in enumerate(PARTS):
-            outb[pl.ds(part * 16, count), fine(part), half] = gathered[0:count, part]
+        for part, (first, count) in enumerate(PARTS):
+            outb[pl.ds(first, count), fine(part), half] = gathered[first : first + count]
 
     def strip(part, step, lanes):
         (place, length), _ = axes(part)
         rows = 256 // length
-        return pl.ds(part * 16, PARTS[part][1]), span(ahead(place, -step, length) * rows, rows), lanes
+        return pl.ds(*PARTS[part]), span(ahead(place, -step, length) * rows, rows), lanes
 
     def hand_over(part, step):
         copy = push(strip(part, step, half), a0_s.at[part, step], a0_r.at[part, step], sister)
@@ -465,6 +475,131 @@
             for part in range(2):
                 if step < axes(part)[0][1]:
                     push(strip(part, step, other_half), a0_s.at[part, step], a0_r.at[part, step], here).wait_recv()
+
+    rows_x, mine_z = 256 // X, first_z + slot
+
+    def toward(i):
+        steps = lax.rem(owners[i] + Z - z, Z)
+        place = jnp.maximum(steps - 1, 0)
+        return remote(s1.at[first_z + i], rz.at[place], z1_s.at[i], z1_r.at[place], device(jnp.int32(owners[i]), x, y, c))
+
+    def along_x(step):
+        return remote(s2z.at[span(ahead(x, step, X) * rows_x, rows_x)], r2z.at[step - 1], z2_s.at[step - 1],
+                      z2_r.at[step - 1], device(z, ahead(x, step, X), y, c))
+
+    def along_y(step):
+        return remote(s3z.at[span(ahead(y, step, Y) * small, small)], r3z.at[step - 1], z3_s.at[step - 1],
+                      z3_r.at[step - 1], device(z, x, ahead(y, step, Y), c))
+
+    def back_y(step, behind):
+        rows = span(x * rows_x + ahead(y, -behind, Y) * small, small)
+        return push((mine_z, rows, half), b3_s.at[step - 1], b3_r.at[step - 1], device(z, x, ahead(y, step, Y), c))
+
+    def back_x(step, behind):
+        rows = span(ahead(x, -behind, X) * rows_x, rows_x)
+        return push((mine_z, rows, half), b2_s.at[step - 1], b2_r.at[step - 1], device(z, ahead(x, step, X), y, c))
+
+    def back_z(dz):
+        return push((mine_z, pl.ds(0, 256), half), b1_s.at[dz - 1], b1_r.at[slot], device(ahead(z, dz, Z), x, y, c))
+
+    def products_z():
+        for k in range(first_z, first_z + count_z):
+            own[k] = dot(cols_t[k], half_grads[0])
+
+    def stage1_z():
+        for i in range(count_z):
+            k = first_z + i
+            value = own[k] + dot(cols_sister[k], half_grads[2])
+            own[k] = value
+            s1[k] = value.astype(BF16)
+
+            @pl.when(z != owners[i])
+            def _():
+                toward(i).start()
+
+    def stage2_z():
+        @pl.when(is_owner)
+        def _():
+            value = own[mine_z]
+            for place in range(Z - 1):
+                remote(s1.at[first_z], rz.at[place], z1_s.at[0], z1_r.at[place], here).wait_recv()
+                value = value + rz[place].astype(F32)
+            own2z[...] = value
+            s2z[...] = value.astype(BF16)
+            for step in far_first(X):
+                along_x(step).start()
+
+    def stage3_z():
+        @pl.when(is_owner)
+        def _():
+            value = own2z[span(x * rows_x, rows_x), :]
+            for step in far_first(X):
+                along_x(step).wait_recv()
+                value = value + r2z[step - 1].astype(F32)
+            own3z[...] = value
+            s3z[...] = value.astype(BF16)
+            for step in far_first(Y):
+                along_y(step).start()
+
+    def back3_z():
+        @pl.when(is_owner)
+        def _():
+            value = own3z[span(y * small, small), :]
+            for step in far_first(Y):
+                along_y(step).wait_recv()
+                value = value + r3z[step - 1].astype(F32)
+            outb[mine_z, span(x * rows_x + y * small, small), half] = (value * inverse_root[:, :128]).astype(BF16)
+            for step in far_first(Y):
+                back_y(step, 0).start()
+
+    def back2_z():
+        @pl.when(is_owner)
+        def _():
+            for step in far_first(Y):
+                back_y(step, step).wait_recv()
+            for step in far_first(X):
+                back_x(step, 0).start()
+
+    def back1_z():
+        @pl.when(is_owner)
+        def _():
+            for step in far_first(X):
+                back_x(step, step).wait_recv()
+            for dz in far_first(Z):
+                back_z(dz).start()
+
+    def offset_z(i, lanes, send, receive, to):
+        return push((first_z + i, pl.ds(0, 256), lanes), send, receive, to)
+
+    def back0_z():
+        for i in range(count_z):
+            @pl.when(z != owners[i])
+            def _():
+                offset_z(i, half, b1_s.at[0], b1_r.at[i], here).wait_recv()
+
+            copy = offset_z(i, half, b0_s.at[i], b0_r.at[i], sister)
+            copy.start()
+            sent.append(copy)
+
+    def finish_z():
+        for i in range(count_z):
+            @pl.when(z != owners[i])
+            def _():
+                toward(i).wait_send()
+
+        @pl.when(is_owner)
+        def _():
+            for step in range(1, X):
+                along_x(step).wait_send()
+                back_x(step, 0).wait_send()
+            for step in range(1, Y):
+                along_y(step).wait_send()
+                back_y(step, 0).wait_send()
+            for dz in range(1, Z):
+                back_z(dz).wait_send()
+
+        for i in range(count_z):
+            offset_z(i, other_half, b0_s.at[i], b0_r.at[i], here).wait_recv()
 
     def column_grads():
         grad_s[...] = jnp.zeros_like(grad_s)
@@ -503,17 +638,18 @@
             fgrad_ref[b] = (extra * occ_brick[rows]).astype(BF16)
 
     schedule = (
-        (products, 0), (products, 1), (hear_sister,),
-        (stage1, 0), (stage1, 1),
+        (products, 0), (products, 1), (products_z,), (hear_sister,),
+        (stage1, 0), (stage1, 1), (stage1_z,),
         (products, 2), (products, 3), (stage1, 2), (stage1, 3),
         (column_grads,), (settle,),
-        (stage2, 0), (stage2, 1), (stage3,),
-        (brick_grads,), (back3,),
-        (feature_grads,),
-        (back2,),
-        (back1, 0), (back1, 1),
+        (stage2, 0), (stage2, 1), (stage2_z,),
+        (stage3,), (stage3_z,),
+        (brick_grads,),
+        (back3_z,), (back3,),
+        (back2_z,), (feature_grads,), (back2,),
+        (back1_z,), (back1, 0), (back1, 1),
         (settle,),
-        (back0,), (finish,), (settle,),
+        (back0,), (back0_z,), (finish,), (finish_z,), (settle,),
     )
     for step, *piece in schedule:
         step(*piece)
@@ -521,8 +657,7 @@
 
 def write_out(block, fgrad, wgrad, ggrad, bgrad, block_out, fgrad_out, wgrad_out, ggrad_out, bgrad_out, sems):
     pairs = [(block, block_out), (fgrad, fgrad_out), (ggrad, ggrad_out), (bgrad, bgrad_out)]
-    for part, (first, count) in enumerate(PARTS):
-        pairs.append((wgrad.at[pl.ds(part * 16, count)], wgrad_out.at[pl.ds(first, count)]))
+    pairs.append((wgrad, wgrad_out))
     copies = [pltpu.make_async_copy(source, target, sems.at[i]) for i, (source, target) in enumerate(pairs)]
     for copy in copies:
         copy.start()
@@ -534,7 +669,8 @@
     vmem = pl.BlockSpec(memory_space=pltpu.VMEM)
     small = 256 // (X * Y)
     near, far = max(X, Y) - 1, Z - 1
-    depth = 16 // Z
+    depth = slots() // Z
+    third = THIRD[1]
     pieces = len(PIECES)
     dma = pltpu.SemaphoreType.DMA
     scratch = [
@@ -572,10 +708,17 @@
         pltpu.VMEM((near, 27, 256 // min(X, Y), 128), BF16),
         pltpu.VMEM((27, 256 // min(X, Y), 128), BF16),
         pltpu.VMEM((near, 27, small, 128), BF16),
-        pltpu.VMEM((16, 2, small, 128), BF16),
-        pltpu.VMEM((16, 2, small, 128), F32),
-        pltpu.VMEM((far, depth, 2, small, 128), BF16),
-        pltpu.VMEM((16, 2, small, 128), BF16),
+        pltpu.VMEM((slots(), small, 128), BF16),
+        pltpu.VMEM((slots(), small, 128), F32),
+        pltpu.VMEM((far, depth, small, 128), BF16),
+        pltpu.VMEM((slots(), small, 128), BF16),
+        pltpu.VMEM((far, 256, 128), BF16),
+        pltpu.VMEM((256, 128), F32),
+        pltpu.VMEM((256, 128), BF16),
+        pltpu.VMEM((near, 256 // X, 128), BF16),
+        pltpu.VMEM((256 // X, 128), F32),
+        pltpu.VMEM((256 // X, 128), BF16),
+        pltpu.VMEM((near, small, 128), BF16),
         dma((7,)), dma((8,)), dma((8,)),
         dma((2 * Z - 1,)), dma((2 * Z - 1,)), dma((X * Y - 1,)), dma((X * Y - 1,)),
         dma((2 * Z - 1,)), dma((2 * Z - 1,)), dma((X * Y - 1,)), dma((X * Y - 1,)),
@@ -583,6 +726,8 @@
         dma((pieces, near)), dma((pieces, near)), dma((2, near)), dma((2, near)), dma((far,)), dma((far,)),
         dma((far,)), dma((far,)), dma((2, near)), dma((2, near)),
         dma((2, near)), dma((2, near)), dma((2, near + 1)), dma((2, near + 1)),
+        dma((third,)), dma((far,)), dma((near,)), dma((near,)), dma((near,)), dma((near,)),
+        dma((near,)), dma((near,)), dma((near,)), dma((near,)), dma((far,)), dma((third,)), dma((third,)), dma((third,)),
     ]
     anywhere = pl.BlockSpec(memory_space=pl.ANY)
     results = pl.pallas_call(
@@ -591,7 +736,7 @@
         out_shape=(
             pltpu.VMEM((4, 64, 256), BF16),
             pltpu.VMEM((4, 64, 256), BF16),
-            pltpu.VMEM((32, 256, 256), BF16),
+            pltpu.VMEM((27, 256, 256), BF16),
             pltpu.VMEM((1, 256), F32),
             pltpu.VMEM((1, 256), F32),
         ),
@@ -613,7 +758,7 @@
         ),
         in_specs=[anywhere] * 5,
         out_specs=(anywhere,) * 5,
-        scratch_shapes=[dma((6,))],
+        scratch_shapes=[dma((5,))],
         compiler_params=pltpu.CompilerParams(vmem_limit_bytes=8 * 2**20),
     )(*results)
     return block, fgrad, wgrad, ggrad.reshape(256), bgrad.reshape(256)

time: 94.5 us -> 89.4 us (0.946)
  Pallas kernels: 93.7 us -> 88.5 us
    pallas_call x1, Pallas kernels: 91.8 us -> 86.6 us  [on_device(): pl.pallas_call(kernel, name='brick_block', out_shape=(pltpu.VMEM((4, 64,...]
where the time goes in v4:
time: 89.4 us; the launch traced here: 89.3 us
  Pallas kernels  88.5 us (99%)
    pallas_call x1, Pallas kernels, on_device(): pl.pallas_call(kernel, name='brick_block', out_shape=(pltpu.VMEM((4, 64,...  86.6 us
    pallas_call x1, Pallas kernels, on_device(): pl.pallas_call(write_out, name='write_out', out_shape=(jax.ShapeDtypeStru...  1.93 us

profile of v4, /device:TPU:1, one launch (start us, length us, event | category | flops | bytes accessed | tf_op | source)
XLA Modules:
  0.0 89.3 jit_solution(16910016320121550810)
XLA Ops:
  0.6 86.6 %brick_block.1 = (bf16[4,64,256]{2,1,0:T(8,128)(2,1)S(1)}, bf16[4,64,256]{2,1,0:T(8,128)(2,1)S(1)}, bf16[27,256,256]{2,1,0:T(8,128)(2,1)S(1)}, f32[1,256]{1,0:T(1,128)S(1)}, f32[1,256]{1,0:T(1,128)S(1)}) custom-call(s32[4,64]{1,0:T(4,128)} %occ_hbm.1, s32[4,27]{1,0:T(4,128)} %nb_hbm.1, s32[1,8]{1,0:T(1,128)} %bitcast.7, bf16[4,64,256]{2,1,0:T(8,128)(2,1)} %feat_hbm.1, ...), custom_call_target="tpu_custom_call" | custom-call | tf_op jit(solution)/shard_map/brick_block/pallas_call | solution.py:733
  87.2 1.9 %write_out.1 = (bf16[4,64,256]{2,1,0:T(8,128)(2,1)}, bf16[4,64,256]{2,1,0:T(8,128)(2,1)}, bf16[27,256,256]{2,1,0:T(8,128)(2,1)}, f32[1,256]{1,0:T(1,128)}, f32[1,256]{1,0:T(1,128)}) custom-call(bf16[4,64,256]{2,1,0:T(8,128)(2,1)S(1)} %get-tuple-element.15.block, bf16[4,64,256]{2,1,0:T(8,128)(2,1)S(1)} %get-tuple-element.16.fgrad, ...), custom_call_target="tpu_custom_call" | custom-call | tf_op jit(solution)/shard_map/write_out/pallas_call | solution.py:749

commit v5 on v4

--- a/solution.py
+++ b/solution.py
@@ -646,9 +646,9 @@
         (stage3,), (stage3_z,),
         (brick_grads,),
         (back3_z,), (back3,),
-        (back2_z,), (feature_grads,), (back2,),
+        (back2_z,), (back2,),
         (back1_z,), (back1, 0), (back1, 1),
-        (settle,),
+        (feature_grads,), (settle,),
         (back0,), (back0_z,), (finish,), (finish_z,), (settle,),
     )
     for step, *piece in schedule:

time: 89.4 us -> 88.5 us (0.990)
  Pallas kernels: 88.5 us -> 87.6 us
where the time goes in v5:
time: 88.5 us; the launch traced here: 88.4 us
  Pallas kernels  87.6 us (99%)
    pallas_call x1, Pallas kernels, on_device(): pl.pallas_call(kernel, name='brick_block', out_shape=(pltpu.VMEM((4, 64,...  85.7 us
    pallas_call x1, Pallas kernels, on_device(): pl.pallas_call(write_out, name='write_out', out_shape=(jax.ShapeDtypeStru...  1.93 us

profile of v5, /device:TPU:1, one launch (start us, length us, event | category | flops | bytes accessed | tf_op | source)
XLA Modules:
  0.0 88.4 jit_solution(2876487712917879875)
XLA Ops:
  0.6 85.7 %brick_block.1 = (bf16[4,64,256]{2,1,0:T(8,128)(2,1)S(1)}, bf16[4,64,256]{2,1,0:T(8,128)(2,1)S(1)}, bf16[27,256,256]{2,1,0:T(8,128)(2,1)S(1)}, f32[1,256]{1,0:T(1,128)S(1)}, f32[1,256]{1,0:T(1,128)S(1)}) custom-call(s32[4,64]{1,0:T(4,128)} %occ_hbm.1, s32[4,27]{1,0:T(4,128)} %nb_hbm.1, s32[1,8]{1,0:T(1,128)} %bitcast.7, bf16[4,64,256]{2,1,0:T(8,128)(2,1)} %feat_hbm.1, ...), custom_call_target="tpu_custom_call" | custom-call | tf_op jit(solution)/shard_map/brick_block/pallas_call | solution.py:733
  86.3 1.9 %write_out.1 = (bf16[4,64,256]{2,1,0:T(8,128)(2,1)}, bf16[4,64,256]{2,1,0:T(8,128)(2,1)}, bf16[27,256,256]{2,1,0:T(8,128)(2,1)}, f32[1,256]{1,0:T(1,128)}, f32[1,256]{1,0:T(1,128)}) custom-call(bf16[4,64,256]{2,1,0:T(8,128)(2,1)S(1)} %get-tuple-element.15.block, bf16[4,64,256]{2,1,0:T(8,128)(2,1)S(1)} %get-tuple-element.16.fgrad, ...), custom_call_target="tpu_custom_call" | custom-call | tf_op jit(solution)/shard_map/write_out/pallas_call | solution.py:749

commit v6 on v5

--- a/solution.py
+++ b/solution.py
@@ -17,7 +17,7 @@
 F32, BF16, I32 = jnp.float32, jnp.bfloat16, jnp.int32
 
 PARTS = ((0, 11), (11, 11))
-PIECES = ((0, 5, 0), (11, 5, 1), (5, 6, 0), (16, 6, 1))
+PIECES = ((0, 3, 0), (11, 3, 1), (3, 8, 0), (14, 8, 1))
 THIRD = (22, 5)
 
 

time: 88.5 us -> 88.8 us (level)
  no operation moved by 1% of the time
where the time goes in v6:
time: 88.8 us; the launch traced here: 88.7 us
  Pallas kernels  87.9 us (99%)
    pallas_call x1, Pallas kernels, on_device(): pl.pallas_call(kernel, name='brick_block', out_shape=(pltpu.VMEM((4, 64,...  86 us
    pallas_call x1, Pallas kernels, on_device(): pl.pallas_call(write_out, name='write_out', out_shape=(jax.ShapeDtypeStru...  1.93 us

profile of v6, /device:TPU:1, one launch (start us, length us, event | category | flops | bytes accessed | tf_op | source)
XLA Modules:
  0.0 88.7 jit_solution(989623558211835730)
XLA Ops:
  0.6 86.0 %brick_block.1 = (bf16[4,64,256]{2,1,0:T(8,128)(2,1)S(1)}, bf16[4,64,256]{2,1,0:T(8,128)(2,1)S(1)}, bf16[27,256,256]{2,1,0:T(8,128)(2,1)S(1)}, f32[1,256]{1,0:T(1,128)S(1)}, f32[1,256]{1,0:T(1,128)S(1)}) custom-call(s32[4,64]{1,0:T(4,128)} %occ_hbm.1, s32[4,27]{1,0:T(4,128)} %nb_hbm.1, s32[1,8]{1,0:T(1,128)} %bitcast.7, bf16[4,64,256]{2,1,0:T(8,128)(2,1)} %feat_hbm.1, ...), custom_call_target="tpu_custom_call" | custom-call | tf_op jit(solution)/shard_map/brick_block/pallas_call | solution.py:733
  86.6 1.9 %write_out.1 = (bf16[4,64,256]{2,1,0:T(8,128)(2,1)}, bf16[4,64,256]{2,1,0:T(8,128)(2,1)}, bf16[27,256,256]{2,1,0:T(8,128)(2,1)}, f32[1,256]{1,0:T(1,128)}, f32[1,256]{1,0:T(1,128)}) custom-call(bf16[4,64,256]{2,1,0:T(8,128)(2,1)S(1)} %get-tuple-element.15.block, bf16[4,64,256]{2,1,0:T(8,128)(2,1)S(1)} %get-tuple-element.16.fgrad, ...), custom_call_target="tpu_custom_call" | custom-call | tf_op jit(solution)/shard_map/write_out/pallas_call | solution.py:749
